TPU v7x, 32 devices: a whole 2x2x4 slice. The times are simulated.
32 devices in a mesh: dp: 2 (over x), expert: 16 (over z, y, core).
Axes of the slice: x: 2, y: 2, z: 4, core: 2. Of those that a mesh axis runs over, the one named last changes fastest.
Arguments:
- tokens: bfloat16 [512, 4096], P(('dp', 'expert')), may hold values from -6 to 6
- route_ids: int32 [512, 8], P(('dp', 'expert')), may hold values from 0 to 31, all different within a row; in each aligned block of 16 rows (0 to 15, 16 to 31, ...) at most 8 rows name the same one
- gate_weights: float32 [512, 8], P(('dp', 'expert')), may hold values from 0.05 to 0.3
- tenant_ids: int32 [512], P(('dp', 'expert')), may hold values from 0 to 3
- up_weight: bfloat16 [32, 4096, 1024], P('expert', 'dp'), may hold values from -0.09375 to 0.09375
- down_weight: bfloat16 [32, 1024, 4096], P('expert', None, 'dp'), may hold values from -0.1875 to 0.1875
- adapter_in: bfloat16 [32, 4096, 64], P('expert', 'dp'), may hold values from -0.09375 to 0.09375
- adapter_out: bfloat16 [32, 64, 1024], P('expert'), may hold values from -1.5 to 1.5
Outputs:
- mixed: bfloat16 [512, 4096], P(('dp', 'expert'))
Inputs may be any that keep to these rules, and one draw needn't show every extreme that they name: `route_ids`: the 8 experts of one token differ; among the 16 tokens of one device no expert is named more than 8 times, and some expert is named 8 times.
All inputs are finite; a program needn't handle non-finite values.
Results may differ from a plain program's by a relative error of at most 0.025.
Values may be sent and summed in bfloat16 or wider, within the bound.
A program may use at most 64 MiB of HBM per device.

v0:
```python
import jax
import jax.numpy as jnp
from jax import lax
from jax.sharding import PartitionSpec as P

RANK = 16


def per_device(
    tokens, route_ids, gate_weights, tenant_ids, up_weight, down_weight, adapter_in, adapter_out
):
    n_dp = lax.axis_size("dp")
    n_col = lax.axis_size("expert")
    tok_count = tokens.shape[0]
    chosen = route_ids.shape[1]
    features = tokens.shape[1]
    exp_local = up_weight.shape[0]
    piece = up_weight.shape[1]
    units = up_weight.shape[2]
    adapter_cols = adapter_in.shape[2]
    experts_all = exp_local * n_col
    capacity = max(2, 2 * tok_count * chosen // experts_all)
    send_rows = experts_all * capacity
    flat_routes = route_ids.reshape(-1)
    order = jnp.arange(flat_routes.shape[0], dtype=jnp.int32)
    same = flat_routes[:, None] == flat_routes[None, :]
    earlier = order[None, :] < order[:, None]
    rank = jnp.sum((same & earlier).astype(jnp.int32), axis=1)
    target = flat_routes * capacity + rank
    outgoing = (
        jnp.zeros((send_rows, features), jnp.bfloat16)
        .at[target]
        .set(jnp.repeat(tokens, chosen, axis=0))
    )
    tag_line = (
        jnp.full((send_rows,), -1.0, jnp.float32)
        .at[target]
        .set(jnp.repeat(tenant_ids, chosen).astype(jnp.float32))
    )
    tag_grid = jnp.broadcast_to(tag_line[:, None], (send_rows, n_dp)).astype(jnp.bfloat16)
    sending = outgoing.reshape(n_col, exp_local, capacity, n_dp, piece)
    tag_send = tag_grid.reshape(n_col, exp_local, capacity, n_dp, 1)
    arrived, arrived_tags = (
        lax.all_to_all(
            lax.all_to_all(sending, "dp", split_axis=3, concat_axis=2, tiled=True),
            "expert",
            split_axis=0,
            concat_axis=2,
            tiled=True,
        ),
        lax.all_to_all(
            lax.all_to_all(tag_send, "dp", split_axis=3, concat_axis=2, tiled=True),
            "expert",
            split_axis=0,
            concat_axis=2,
            tiled=True,
        ),
    )
    rows_all = arrived.shape[2]
    grid = arrived.reshape(exp_local, rows_all, piece)
    tags = arrived_tags.reshape(exp_local, rows_all).astype(jnp.float32)
    up_part = jnp.einsum("erd,edf->erf", grid, up_weight, preferred_element_type=jnp.float32)
    shrink_part = jnp.einsum("erd,edl->erl", grid, adapter_in, preferred_element_type=jnp.float32)
    owner = (jnp.arange(adapter_cols, dtype=jnp.int32) // RANK).astype(jnp.float32)
    shrink = lax.psum(shrink_part.astype(jnp.bfloat16), "dp").astype(jnp.float32)
    keep = owner[None, None, :] == tags[..., None]
    masked_values = jnp.where(keep, shrink, jnp.zeros((), jnp.float32))
    up_portion = lax.psum_scatter(
        up_part.astype(jnp.bfloat16), "dp", scatter_dimension=2, tiled=True
    ).astype(jnp.float32)
    share = units // n_dp
    mapping_portion = lax.dynamic_slice_in_dim(
        adapter_out, lax.axis_index("dp") * share, share, 2
    ).astype(jnp.float32)
    low_rank_adapter = jnp.einsum(
        "erl,elf->erf", masked_values, mapping_portion, precision=lax.Precision.HIGHEST
    )
    hidden_portion = jax.nn.silu(up_portion + low_rank_adapter).astype(jnp.bfloat16)
    hidden_activations = lax.all_gather(hidden_portion, "dp", axis=2, tiled=True)
    expert_out = jnp.einsum(
        "erf,efd->erd", hidden_activations, down_weight, preferred_element_type=jnp.float32
    ).astype(jnp.bfloat16)
    going_back = expert_out.reshape(1, exp_local, rows_all, 1, piece)
    returned = lax.all_to_all(
        lax.all_to_all(going_back, "expert", split_axis=2, concat_axis=0, tiled=True),
        "dp",
        split_axis=2,
        concat_axis=3,
        tiled=True,
    )
    results = returned.reshape(send_rows, features)
    picked = results[target].astype(jnp.float32).reshape(tok_count, chosen, features)
    mixed = jnp.sum(picked * gate_weights[:, :, None], axis=1)
    return mixed.astype(jnp.bfloat16)


def solution(mesh):
    placed = (
        P(("dp", "expert"), None),
        P(("dp", "expert"), None),
        P(("dp", "expert"), None),
        P(("dp", "expert")),
        P("expert", "dp", None),
        P("expert", None, "dp"),
        P("expert", "dp", None),
        P("expert", None, None),
    )
    return jax.shard_map(
        per_device, mesh=mesh, in_specs=placed, out_specs=P(("dp", "expert"), None), check_vma=False
    )
```

profile of v0, /device:TPU:0, one launch (start us, length us, event | category | flops | bytes accessed | tf_op | source)
XLA Modules:
  0.0 277.0 jit_solution(423219524754056762)
XLA Ops:
  6.5 0.0 copy-start
  6.5 0.0 all-reduce.2.cloned.1.call-start
  6.5 0.7 broadcast_multiply_fusion
  7.3 0.8 copy.41
  8.0 0.1 copy.40
  8.1 0.1 mul.33
  8.2 0.1 eq.28
  8.3 0.2 convert_reduce_fusion
  8.5 3.1 %scatter_custom_fusion = bf16[256,4096]{1,0:T(8,128)(2,1)S(1)} fusion(s32[128]{0:T(128)S(1)} %fusion.15, bf16[]{:T(256)} %constant.13.clone.1, bf16[16,4096]{1,0:T(8,128)(2,1)} %param.8), kind=kCustom, calls=%fused_computation.12 | custom fusion | bytes 2228226 | tf_op jit(solution)/shard_map/scatter | solution.py:33
  11.6 2.8 reshape.88
  14.4 2.5 copy.42
  16.8 28.9 %all_to_all.93 = bf16[16,2,8,2,2048]{4,2,1,0,3:T(8,128)(2,1)S(1)} all-to-all(bf16[16,2,8,2,2048]{4,2,1,0,3:T(8,128)(2,1)S(1)} %copy.42), channel_id=1, replica_groups=mesh['dp'=2,'expert'=16] {'dp'}, dimensions={3} | all-to-all | bytes 4194304 | tf_op jit(solution)/shard_map/all_to_all | solution.py:45
  45.7 0.2 copy.58
  45.9 53.3 %all_to_all.94 = bf16[16,2,16,1,2048]{4,2,1,3,0:T(8,128)(2,1)S(1)} all-to-all(bf16[16,2,16,1,2048]{4,2,1,3,0:T(8,128)(2,1)S(1)} %bitcast.68), channel_id=1, replica_groups=mesh['dp'=2,'expert'=16] {'expert'}, dimensions={0} | all-to-all | bytes 4194304 | tf_op jit(solution)/shard_map/all_to_all | solution.py:44
  99.2 0.1 copy.45
  99.4 0.0 copy-done
  99.4 1.4 convolution_convert_fusion.2
  100.8 0.0 all-reduce.2.cloned.1.call-update
  100.8 0.0 copy-start.4
  100.8 0.0 copy-start.3
  100.8 0.0 reduce-scatter.2.cloned.1.call-start
  100.9 6.7 %convolution_convert_fusion.1 = bf16[2,256,1024]{2,1,0:T(8,128)(2,1)} fusion(bf16[2,256,2048]{2,1,0:T(8,128)(2,1)S(1)} %bitcast.65, bf16[2,2048,1024]{2,1,0:T(8,128)(2,1)} %param.12), kind=kOutput, calls=%fused_computation.9 | convolution fusion | flops 2148007936 | bytes 11534336 | tf_op jit(solution)/shard_map/erd,edf->erf/dot_general | solution.py:62
  107.6 0.0 reduce-scatter.2.cloned.1.call-update
  107.6 0.0 copy-done.4
  107.7 0.1 broadcast_in_dim.35
  107.7 0.1 reshape.115
  107.8 1.0 scatter_custom_fusion.1
  108.8 0.1 broadcast_in_dim.36
  108.9 0.1 copy.46
  109.0 0.1 reshape.123
  109.1 6.1 %all_to_all.95 = bf16[2,2,128]{2,1,0:T(2,128)(2,1)S(1)} all-to-all(bf16[2,2,128]{2,1,0:T(2,128)(2,1)S(1)} %reshape.123), channel_id=1, replica_groups=mesh['dp'=2,'expert'=16] {'dp'}, dimensions={0} | all-to-all | bytes 2048 | tf_op jit(solution)/shard_map/all_to_all | solution.py:52
  115.2 0.1 reshape.124
  115.3 0.7 copy.48
  115.9 5.1 %all-to-all-start.3 = ((bf16[16,2,16,1,1]{2,1,4,3,0:T(2,128)(2,1)}), bf16[16,2,16,1,1]{2,1,4,3,0:T(2,128)(2,1)S(1)}, u32[]{:S(2)}, u32[]{:S(2)}) async-start(bf16[16,2,16,1,1]{2,1,4,3,0:T(2,128)(2,1)} %copy.48), calls=%async_computation.4 | async-start | bytes 16384 | tf_op jit(solution)/shard_map/all_to_all | solution.py:51
  121.1 0.2 all-gather.2.cloned.1.call-start
  121.3 6.2 %all-to-all-done.3 = bf16[16,2,16,1,1]{2,1,4,3,0:T(2,128)(2,1)S(1)} async-done(((bf16[16,2,16,1,1]{2,1,4,3,0:T(2,128)(2,1)}), bf16[16,2,16,1,1]{2,1,4,3,0:T(2,128)(2,1)S(1)}, u32[]{:S(2)}, u32[]{:S(2)}) %all-to-all-start.3) | async-done | bytes 1056 | tf_op jit(solution)/shard_map/all_to_all | solution.py:51
  127.5 0.1 reshape.92
  127.6 0.0 all-reduce.2.cloned.1.call-done
  127.6 16.3 %reduce-scatter.2.cloned.1.call-done = bf16[2,256,512]{2,1,0:T(8,128)(2,1)} async-done(((bf16[2,256,1024]{2,1,0:T(8,128)(2,1)}), bf16[2,256,512]{2,1,0:T(8,128)(2,1)}) %reduce-scatter.2.cloned.1.call-update) | async-done | bytes 524304 | tf_op jit(solution)/shard_map/reduce_scatter | solution.py:68
  143.8 0.0 copy-done.3
  143.8 2.8 %multiply_convert_fusion = bf16[2,256,512]{2,1,0:T(8,128)(2,1)} fusion(bf16[2,256,512]{2,1,0:T(8,128)(2,1)} %reduce-scatter.2.cloned.1.call-done, bf16[2,64,1024]{2,1,0:T(8,128)(2,1)S(1)} %copy-done.3, s32[]{:T(128)S(6)} %select_n.31, bf16[2,256,64]{1,2,0:T(8,128)(2,1)} %all-reduce.2.cloned.1.call-done, f32[2,256]{1,0:T(2,128)S(1)} %reshape.92, ...), kind=kOutput, calls=%fused_computation.14 | convolution fusion | flops 203259904 | bytes 1247748 | tf_op jit(solution)/shard_map/erl,elf->erf/dot_general | solution.py:75
  146.6 0.0 all-gather.2.cloned.1.call-update
  146.7 21.5 %all-gather.2.cloned.1.call-done = bf16[2,256,1024]{2,1,0:T(8,128)(2,1)} async-done(((bf16[2,256,512]{2,1,0:T(8,128)(2,1)}), bf16[2,256,1024]{2,1,0:T(8,128)(2,1)}) %all-gather.2.cloned.1.call-update) | async-done | bytes 1048592 | tf_op jit(solution)/shard_map/all_gather | solution.py:79
  168.1 6.1 %fusion = bf16[1,2,256,1,2048]{4,2,1,3,0:T(8,128)(2,1)S(1)} fusion(bf16[2,256,1024]{2,1,0:T(8,128)(2,1)} %all-gather.2.cloned.1.call-done, bf16[2,1024,2048]{2,1,0:T(8,128)(2,1)} %param.13), kind=kOutput, calls=%fused_computation.4 | convolution fusion | flops 2148532224 | bytes 11534336 | tf_op jit(solution)/shard_map/erf,efd->erd/dot_general | solution.py:80
  174.2 2.2 copy.50
  176.3 52.7 %all_to_all.96 = bf16[1,2,256,1,2048]{4,1,3,0,2:T(2,128)(2,1)S(1)} all-to-all(bf16[1,2,256,1,2048]{4,1,3,0,2:T(2,128)(2,1)S(1)} %copy.50), channel_id=1, replica_groups=mesh['dp'=2,'expert'=16] {'expert'}, dimensions={2} | all-to-all | bytes 4194304 | tf_op jit(solution)/shard_map/all_to_all | solution.py:85
  229.1 2.5 copy.57
  231.6 0.0 copy-start.2
  231.6 3.9 %all-to-all-start.5 = ((bf16[16,2,16,1,2048]{4,0,1,3,2:T(8,128)(2,1)}), bf16[16,2,16,1,2048]{4,0,1,3,2:T(8,128)(2,1)S(1)}, u32[]{:S(2)}, u32[]{:S(2)}) async-start(bf16[16,2,16,1,2048]{4,0,1,3,2:T(8,128)(2,1)} %bitcast.67), calls=%async_computation.6 | async-start | bytes 4194304 | tf_op jit(solution)/shard_map/all_to_all | solution.py:84
  235.5 0.0 copy-done.2
  235.5 0.1 copy.53
  235.6 25.9 %all-to-all-done.5 = bf16[16,2,16,1,2048]{4,0,1,3,2:T(8,128)(2,1)S(1)} async-done(((bf16[16,2,16,1,2048]{4,0,1,3,2:T(8,128)(2,1)}), bf16[16,2,16,1,2048]{4,0,1,3,2:T(8,128)(2,1)S(1)}, u32[]{:S(2)}, u32[]{:S(2)}) %all-to-all-start.5) | async-done | bytes 2097184 | tf_op jit(solution)/shard_map/all_to_all | solution.py:84
  261.5 0.0 copy-start.1
  261.5 1.3 copy-done.1
  262.8 2.7 copy.52
  265.6 2.2 gather_fusion
  267.7 2.7 fusion.1
  (9 shorter events, 0.0 us)
Async XLA Ops:
  6.5 92.9 %copy-start = (bf16[2,2048,64]{1,2,0:T(8,128)(2,1)S(1)}, bf16[2,2048,64]{1,2,0:T(8,128)(2,1)}, u32[]{:S(2)}) copy-start(bf16[2,2048,64]{1,2,0:T(8,128)(2,1)} %param.14) | copy-start | bytes 1572868
  6.5 121.0 %all-reduce.2.cloned.1.call-start = ((), (), s32[]{:S(2)}) async-start(), calls=%async_computation.8 | async-start | bytes 131072 | tf_op jit(solution)/shard_map/psum | solution.py:65
  100.8 6.8 %copy-start.4 = (s32[16]{0:T(128)S(1)}, s32[16]{0:T(128)}, u32[]{:S(2)}) copy-start(s32[16]{0:T(128)} %param.11) | copy-start | bytes 196
  100.8 43.0 %copy-start.3 = (bf16[2,64,1024]{2,1,0:T(8,128)(2,1)S(1)}, bf16[2,64,1024]{2,1,0:T(8,128)(2,1)}, u32[]{:S(2)}) copy-start(bf16[2,64,1024]{2,1,0:T(8,128)(2,1)} %param.15) | copy-start | bytes 786436
  100.8 43.0 %reduce-scatter.2.cloned.1.call-start = ((), (), s32[]{:S(2)}) async-start(), calls=%async_computation.7 | async-start | bytes 1572864 | tf_op jit(solution)/shard_map/reduce_scatter | solution.py:68
  115.9 11.5 %all-to-all-start.3 = ((bf16[16,2,16,1,1]{2,1,4,3,0:T(2,128)(2,1)}), bf16[16,2,16,1,1]{2,1,4,3,0:T(2,128)(2,1)S(1)}, u32[]{:S(2)}, u32[]{:S(2)}) async-start(bf16[16,2,16,1,1]{2,1,4,3,0:T(2,128)(2,1)} %copy.48), calls=%async_computation.4 | async-start | bytes 16384 | tf_op jit(solution)/shard_map/all_to_all | solution.py:51
  121.1 47.1 %all-gather.2.cloned.1.call-start = ((), (), s32[]{:S(2)}) async-start(), calls=%async_computation.9 | async-start | bytes 1572864 | tf_op jit(solution)/shard_map/all_gather | solution.py:79
  231.6 3.9 %copy-start.2 = (f32[16,8]{0,1:T(8,128)S(1)}, f32[16,8]{0,1:T(8,128)}, u32[]{:S(2)}) copy-start(f32[16,8]{0,1:T(8,128)} %param.10) | copy-start | bytes 1540
  231.6 29.9 %all-to-all-start.5 = ((bf16[16,2,16,1,2048]{4,0,1,3,2:T(8,128)(2,1)}), bf16[16,2,16,1,2048]{4,0,1,3,2:T(8,128)(2,1)S(1)}, u32[]{:S(2)}, u32[]{:S(2)}) async-start(bf16[16,2,16,1,2048]{4,0,1,3,2:T(8,128)(2,1)} %bitcast.67), calls=%async_computation.6 | async-start | bytes 4194304 | tf_op jit(solution)/shard_map/all_to_all | solution.py:84
  261.5 1.3 copy-start.1
Sparse Core Ops, SparseCore 0:
  100.9 20.2 all-reduce.1
  123.5 20.3 reduce-scatter.1
  146.8 21.2 all-gather.1
where the time goes:
time: 278 us; the launch traced here: 277 us
  blocking collectives  141 us (51%)
  waiting for transfers between devices  69.9 us (25%)
  local copies, waits for them, and re-layouts  23 us (8%)
  matrix products  16.9 us (6%)
  between operations  13.3 us (5%)
  starting transfers between devices  9.27 us (3%)
  other arithmetic  3.64 us (1%)
    all_to_all x1, blocking collectives, per_device(): lax.all_to_all(lax.all_to_all(sending, 'dp', split_axis=3, concat_axis=2,...  53.3 us
    all_to_all x1, blocking collectives, per_device(): lax.all_to_all(going_back, 'expert', split_axis=2, concat_axis=0, tiled=T...  52.7 us
    all_to_all x1, blocking collectives, per_device(): lax.all_to_all(sending, 'dp', split_axis=3, concat_axis=2, tiled=True)  28.9 us
    all_to_all x1, waiting for transfers between devices, per_device(): lax.all_to_all(lax.all_to_all(going_back, 'expert', split_axis=2, concat_...  25.9 us
    all_gather x1, waiting for transfers between devices, per_device(): lax.all_gather(hidden_portion, 'dp', axis=2, tiled=True)  21.5 us
    reduce_scatter x1, waiting for transfers between devices, per_device(): lax.psum_scatter(up_part.astype(jnp.bfloat16), 'dp', scatter_dimension=2,...  16.3 us
    dot_general x1, matrix products, per_device(): jnp.einsum('erd,edf->erf', grid, up_weight, preferred_element_type=jnp.fl...  6.72 us
    all_to_all x1, waiting for transfers between devices, per_device(): lax.all_to_all(lax.all_to_all(tag_send, 'dp', split_axis=3, concat_axis=2...  6.16 us
  transfers between devices with their start and end apart: 5, of which 4 were waited for; matrix products, arithmetic and copies ran while one was open for 3% of the time, Pallas kernels for 0%

commit v1 on v0

--- a/solution.py
+++ b/solution.py
@@ -1,9 +1,398 @@
+import functools
+
 import jax
 import jax.numpy as jnp
 from jax import lax
+from jax.experimental import pallas as pl
+from jax.experimental.pallas import tpu as pltpu
 from jax.sharding import PartitionSpec as P
 
 RANK = 16
+MESH = pl.DeviceIdType.MESH
+BF = jnp.bfloat16
+F32 = jnp.float32
+LANES = 128
+NZ = 4
+
+
+def expert_kernel(
+    dims,
+    xe,
+    w_up_hbm,
+    w_down_hbm,
+    a_in_hbm,
+    a_out_hbm,
+    out,
+    w_up,
+    w_down,
+    a_in,
+    a_out,
+    grid,
+    packed,
+    pick,
+    part,
+    peer,
+    rows_out,
+    y_part,
+    core_in,
+    y_send,
+    y_in,
+    z_send,
+    z_in,
+    x_send,
+    x_in,
+    load_sem,
+    tx_s,
+    tx_r,
+    ty_s,
+    ty_r,
+    tz_s,
+    tz_r,
+    tc_s,
+    tc_r,
+    tw_s,
+    tw_r,
+    v_s,
+    v_r,
+    c_s,
+    c_r,
+    y_s,
+    y_r,
+    z_s,
+    z_r,
+    x_s,
+    x_r,
+):
+    tok, cap, piece, units, cols = dims
+    unit = 2 * tok
+    chunk = 2 * NZ * unit
+    rows = (chunk // tok) * cap
+    x = lax.axis_index("dp")
+    e = lax.axis_index("expert")
+    z = e // 4
+    y = (e // 2) % 2
+    c = e % 2
+    x_dev = (1 - x, e)
+    y_dev = (x, z * 4 + (1 - y) * 2 + c)
+    c_dev = (x, z * 4 + y * 2 + (1 - c))
+
+    def z_dev(d):
+        return (x, lax.rem(z + d, NZ) * 4 + y * 2 + c)
+
+    def place(core, zz):
+        return pl.ds(pl.multiple_of((core * NZ + zz) * unit, unit), unit)
+
+    def remote(src, dst, ss, rs, dev):
+        return pltpu.make_async_remote_copy(
+            src_ref=src, dst_ref=dst, send_sem=ss, recv_sem=rs, device_id=dev, device_id_type=MESH
+        )
+
+    loads = [
+        pltpu.make_async_copy(w_up_hbm, w_up, load_sem.at[0]),
+        pltpu.make_async_copy(a_in_hbm, a_in, load_sem.at[1]),
+        pltpu.make_async_copy(a_out_hbm, a_out, load_sem.at[2]),
+        pltpu.make_async_copy(w_down_hbm, w_down, load_sem.at[3]),
+    ]
+    for copy in loads:
+        copy.start()
+
+    barrier = pltpu.get_barrier_semaphore()
+    for dev in [x_dev, y_dev, c_dev] + [z_dev(d) for d in range(1, NZ)]:
+        pl.semaphore_signal(barrier, inc=1, device_id=dev, device_id_type=MESH)
+    pl.semaphore_wait(barrier, 3 + NZ - 1)
+
+    def half(dp):
+        return pl.ds(pl.multiple_of((c * NZ + z) * unit + dp * tok, tok), tok)
+
+    sends = []
+    cp = remote(xe.at[1 - x], grid.at[1, half(x)], tx_s, tx_r, x_dev)
+    cp.start()
+    sends.append(cp)
+    grid[1, half(x), :] = xe[x]
+    remote(xe.at[1 - x], grid.at[1, half(1 - x)], tx_s, tx_r, x_dev).wait_recv()
+
+    own = place(c, z)
+    cp = remote(grid.at[1, own], grid.at[0, own], ty_s.at[0], ty_r.at[0], y_dev)
+    cp.start()
+    sends.append(cp)
+    cp1 = remote(grid.at[1, own], grid.at[1, own], tw_s.at[0], tw_r.at[0], c_dev)
+    cp1.start()
+    sends.append(cp1)
+    cp.wait_recv()
+    for d in (2, 1, 3):
+        cp = remote(grid.at[0, own], grid.at[0, own], tz_s.at[d], tz_r.at[d], z_dev(d))
+        cp.start()
+        sends.append(cp)
+    cp = remote(grid.at[0, own], grid.at[0, own], tc_s.at[0], tc_r.at[0], c_dev)
+    cp.start()
+    sends.append(cp)
+    for d in (1, 3, 2):
+        there = place(c, lax.rem(z + NZ - d, NZ))
+        remote(grid.at[0, there], grid.at[0, there], tz_s.at[d], tz_r.at[d], z_dev(d)).wait_recv()
+        cp = remote(grid.at[0, there], grid.at[0, there], tc_s.at[d], tc_r.at[d], c_dev)
+        cp.start()
+        sends.append(cp)
+        cp = remote(grid.at[0, there], grid.at[1, there], ty_s.at[d], ty_r.at[d], y_dev)
+        cp.start()
+        sends.append(cp)
+
+    def from_core(k, ss, rs):
+        for d in (0, 1, 3, 2):
+            there = place(1 - c, lax.rem(z + NZ - d, NZ))
+            remote(grid.at[k, there], grid.at[k, there], ss.at[d], rs.at[d], c_dev).wait_recv()
+
+    def compact(k):
+        meta = grid[k, :, piece:]
+        eye = (
+            lax.broadcasted_iota(jnp.int32, (LANES, LANES), 0)
+            == lax.broadcasted_iota(jnp.int32, (LANES, LANES), 1)
+        ).astype(F32).astype(BF)
+        flat = lax.dot_general(
+            eye, meta, (((1,), (1,)), ((), ())), preferred_element_type=F32
+        )
+        t0 = lax.broadcasted_iota(jnp.int32, (chunk, chunk), 0)
+        t1 = lax.broadcasted_iota(jnp.int32, (chunk, chunk), 1)
+        before = jnp.where((t0 // tok == t1 // tok) & (t0 < t1), 1.0, 0.0).astype(BF)
+        r0 = lax.broadcasted_iota(jnp.int32, (rows, chunk), 0)
+        r1 = lax.broadcasted_iota(jnp.int32, (rows, chunk), 1)
+        same = r0 // cap == r1 // tok
+        slot = (r0 % cap).astype(F32)
+        for j in range(2):
+            expert = (2 * e + j).astype(F32)
+            named = jnp.sum(jnp.where(flat[0:8] == expert, 1.0, 0.0), axis=0, keepdims=True)
+            named = jnp.broadcast_to(named, (16, chunk))
+            rank = jnp.dot(named.astype(BF), before, preferred_element_type=F32)
+            hit = same & (slot == rank[0:1]) & (named[0:1] > 0.5)
+            pick[k, j * rows : (j + 1) * rows, :] = jnp.where(hit, 1.0, 0.0).astype(BF)
+        width = piece + LANES
+        step = LANES
+
+        def body(n, carry):
+            at = pl.ds(pl.multiple_of(n * step, step), step)
+            packed[k, :, at] = jnp.dot(
+                pick[k], grid[k, :, at], preferred_element_type=F32
+            ).astype(BF)
+            return carry
+
+        lax.fori_loop(0, width // step, body, 0)
+
+    def up(k, j):
+        here = pl.ds(j * rows, rows)
+        low = jnp.dot(packed[k, here, 0:piece], a_in[j], preferred_element_type=F32)
+        tenant = packed[k, here, piece + 24 : piece + 25].astype(F32)
+        owner = (lax.broadcasted_iota(jnp.int32, (rows, cols), 1) // RANK).astype(F32)
+        low = jnp.where(owner == tenant, low, 0.0).astype(BF)
+        step = 256
+
+        def body(n, carry):
+            at = pl.ds(pl.multiple_of(n * step, step), step)
+            value = jnp.dot(
+                packed[k, here, 0:piece], w_up[j, :, at], preferred_element_type=F32
+            )
+            value = value + jnp.dot(low, a_out[j, :, at], preferred_element_type=F32)
+            part[k, j, :, at] = value.astype(BF)
+            return carry
+
+        lax.fori_loop(0, units // step, body, 0)
+        cp = remote(part.at[k, j], peer.at[k, j], v_s.at[k, j], v_r.at[k, j], x_dev)
+        cp.start()
+        return cp
+
+    def down(k, j, cp):
+        cp.wait_recv()
+        here = pl.ds(j * rows, rows)
+        meta = packed[k, here, piece:].astype(F32)
+        expert = (2 * e + j).astype(F32)
+        gates = jnp.where(meta[:, 0:8] == expert, meta[:, 8:16] + meta[:, 16:24], 0.0)
+        gate = jnp.sum(gates, axis=1, keepdims=True)
+        value = part[k, j].astype(F32) + peer[k, j].astype(F32)
+        hidden = (value / (1.0 + jnp.exp(-value))).astype(BF)
+        step = 256
+
+        def body(n, carry):
+            at = pl.ds(pl.multiple_of(n * step, step), step)
+            value = jnp.dot(hidden, w_down[j, :, at], preferred_element_type=F32)
+            rows_out[here, at] = (value * gate).astype(BF)
+            return carry
+
+        lax.fori_loop(0, piece // step, body, 0)
+
+    def spread(k):
+        size = 2 * rows
+        eye = jnp.where(
+            lax.broadcasted_iota(jnp.int32, (chunk, chunk), 0)
+            == lax.broadcasted_iota(jnp.int32, (chunk, chunk), 1),
+            1.0,
+            0.0,
+        ).astype(BF)
+        back = lax.dot_general(
+            eye, pick[k], (((1,), (1,)), ((), ())), preferred_element_type=F32
+        ).astype(BF)
+        step = 256
+
+        def body(n, carry):
+            at = pl.ds(pl.multiple_of(n * step, step), step)
+            y_part[k, :, at] = jnp.dot(
+                back, rows_out[:, at], preferred_element_type=F32
+            ).astype(BF)
+            return carry
+
+        lax.fori_loop(0, piece // step, body, 0)
+        line = NZ * unit
+        theirs = pl.ds(pl.multiple_of((1 - c) * line, line), line)
+        cp = remote(y_part.at[k, theirs], core_in.at[k], c_s.at[k], c_r.at[k], c_dev)
+        cp.start()
+        return cp
+
+    from_core(0, tc_s, tc_r)
+    compact(0)
+    loads[0].wait()
+    loads[1].wait()
+    loads[2].wait()
+    v00 = up(0, 0)
+    for d in (1, 3, 2):
+        there = place(c, lax.rem(z + NZ - d, NZ))
+        remote(grid.at[0, there], grid.at[1, there], ty_s.at[d], ty_r.at[d], y_dev).wait_recv()
+        cp = remote(grid.at[1, there], grid.at[1, there], tw_s.at[d], tw_r.at[d], c_dev)
+        cp.start()
+        sends.append(cp)
+    v01 = up(0, 1)
+    from_core(1, tw_s, tw_r)
+    compact(1)
+    v10 = up(1, 0)
+    v11 = up(1, 1)
+    loads[3].wait()
+    line = NZ * unit
+    mine = pl.ds(pl.multiple_of(c * line, line), line)
+
+    down(0, 0, v00)
+    down(0, 1, v01)
+    cc = spread(0)
+    cc.wait_recv()
+    y_send[...] = (y_part[0, mine].astype(F32) + core_in[0].astype(F32)).astype(BF)
+    cy = remote(y_send, y_in, y_s, y_r, y_dev)
+    cy.start()
+    down(1, 0, v10)
+    down(1, 1, v11)
+    cd = spread(1)
+    cy.wait_recv()
+    cd.wait_recv()
+    z_send[...] = (
+        y_part[1, mine].astype(F32) + core_in[1].astype(F32) + y_in[...].astype(F32)
+    ).astype(BF)
+
+    def spot(zz):
+        return pl.ds(pl.multiple_of(zz * unit, unit), unit)
+
+    zs = []
+    for d in (2, 1, 3):
+        cp = remote(
+            z_send.at[spot(lax.rem(z + d, NZ))], z_in.at[d - 1], z_s.at[d], z_r.at[d], z_dev(d)
+        )
+        cp.start()
+        zs.append(cp)
+    for cp in zs:
+        cp.wait_recv()
+    total = z_send[spot(z)].astype(F32)
+    for d in range(1, NZ):
+        total = total + z_in[d - 1].astype(F32)
+    x_send[...] = total.astype(BF).reshape(2, tok, piece)
+    cx = remote(x_send.at[1 - x], x_in, x_s, x_r, x_dev)
+    cx.start()
+    keep = x_send[x]
+    cx.wait_recv()
+    other = x_in[...]
+    first = x == 0
+    out[:, 0:piece] = jnp.where(first, keep, other)
+    out[:, piece:] = jnp.where(first, other, keep)
+    for cp in sends + [v00, v01, v10, v11, cc, cd, cy, cx] + zs:
+        cp.wait_send()
+
+
+def fused(
+    tokens, route_ids, gate_weights, tenant_ids, up_weight, down_weight, adapter_in, adapter_out
+):
+    tok = tokens.shape[0]
+    piece = up_weight.shape[1]
+    units = up_weight.shape[2]
+    cols = adapter_in.shape[2]
+    experts_all = up_weight.shape[0] * lax.axis_size("expert")
+    cap = max(2, 2 * tok * route_ids.shape[1] // experts_all)
+    high = lax.reduce_precision(gate_weights, 8, 7)
+    meta = jnp.concatenate(
+        [
+            route_ids.astype(F32),
+            high,
+            gate_weights - high,
+            tenant_ids.astype(F32)[:, None],
+            jnp.zeros((tok, LANES - 25), F32),
+        ],
+        axis=1,
+    ).astype(BF)
+    xe = jnp.stack(
+        [
+            jnp.concatenate([tokens[:, :piece], meta], axis=1),
+            jnp.concatenate([tokens[:, piece:], meta], axis=1),
+        ]
+    )
+    unit = 2 * tok
+    chunk = 2 * NZ * unit
+    rows = (chunk // tok) * cap
+    line = NZ * unit
+    dma = pltpu.SemaphoreType.DMA
+    vm = lambda *shape: pltpu.VMEM(shape, BF)
+    any_spec = pl.BlockSpec(memory_space=pl.ANY)
+    vmem_spec = pl.BlockSpec(memory_space=pltpu.VMEM)
+    return pl.pallas_call(
+        functools.partial(expert_kernel, (tok, cap, piece, units, cols)),
+        out_shape=jax.ShapeDtypeStruct(tokens.shape, BF),
+        in_specs=[vmem_spec] + [any_spec] * 4,
+        out_specs=vmem_spec,
+        scratch_shapes=[
+            vm(*up_weight.shape),
+            vm(*down_weight.shape),
+            vm(*adapter_in.shape),
+            vm(*adapter_out.shape),
+            vm(2, chunk, piece + LANES),
+            vm(2, 2 * rows, piece + LANES),
+            vm(2, 2 * rows, chunk),
+            vm(2, 2, rows, units),
+            vm(2, 2, rows, units),
+            vm(2 * rows, piece),
+            vm(2, chunk, piece),
+            vm(2, line, piece),
+            vm(line, piece),
+            vm(line, piece),
+            vm(line, piece),
+            vm(NZ - 1, unit, piece),
+            vm(2, tok, piece),
+            vm(tok, piece),
+            dma((4,)),
+            dma,
+            dma,
+            dma((NZ,)),
+            dma((NZ,)),
+            dma((NZ,)),
+            dma((NZ,)),
+            dma((NZ,)),
+            dma((NZ,)),
+            dma((NZ,)),
+            dma((NZ,)),
+            dma((2, 2)),
+            dma((2, 2)),
+            dma((2,)),
+            dma((2,)),
+            dma,
+            dma,
+            dma((NZ,)),
+            dma((NZ,)),
+            dma,
+            dma,
+        ],
+        compiler_params=pltpu.CompilerParams(
+            collective_id=0, has_side_effects=True, vmem_limit_bytes=48 * 1024 * 1024
+        ),
+    )(xe, up_weight, down_weight, adapter_in, adapter_out)
 
 
 def per_device(
@@ -105,6 +494,7 @@
         P("expert", "dp", None),
         P("expert", None, None),
     )
+    small = mesh.shape["dp"] == 2 and mesh.shape["expert"] == 4 * NZ
     return jax.shard_map(
-        per_device, mesh=mesh, in_specs=placed, out_specs=P(("dp", "expert"), None), check_vma=False
-    )
+        fused if small else per_device, mesh=mesh, in_specs=placed, out_specs=P(("dp", "expert"), None), check_vma=False
+    )

time: 278 us -> 82.5 us (0.30)
  blocking collectives: 141 us -> 0 us
  Pallas kernels: 0 us -> 74.7 us
  waiting for transfers between devices: 69.9 us -> 0 us
  local copies, waits for them, and re-layouts: 23 us -> 5.89 us
  matrix products: 16.9 us -> 0 us
  between operations: 13.3 us -> 0.04 us
  starting transfers between devices: 9.27 us -> 0 us
    all_to_all x4 -> x0, blocking collectives: 141 us -> none  [the longest x1 53.3 us: per_device(): lax.all_to_all(lax.all_to_all(sending, 'dp', split_axis=3, concat_axis=2,...]
    pallas_call x0 -> x1, Pallas kernels: none -> 74.7 us  [fused(): pl.pallas_call(functools.partial(expert_kernel, (tok, cap, piece, units,...]
    all_to_all x2 -> x0, waiting for transfers between devices: 32.1 us -> none  [the longest x1 25.9 us: per_device(): lax.all_to_all(lax.all_to_all(going_back, 'expert', split_axis=2, concat_...]
    all_gather x1 -> x0, waiting for transfers between devices: 21.5 us -> none  [per_device(): lax.all_gather(hidden_portion, 'dp', axis=2, tiled=True)]
    dot_general x4 -> x0, matrix products: 16.9 us -> none  [the longest x1 6.72 us: per_device(): jnp.einsum('erd,edf->erf', grid, up_weight, preferred_element_type=jnp.fl...]
    reduce_scatter x1 -> x0, waiting for transfers between devices: 16.3 us -> none  [per_device(): lax.psum_scatter(up_part.astype(jnp.bfloat16), 'dp', scatter_dimension=2,...]
    all_to_all x2 -> x0, starting transfers between devices: 9 us -> none  [the longest x1 5.11 us: per_device(): lax.all_to_all(lax.all_to_all(tag_send, 'dp', split_axis=3, concat_axis=2...]
    reshape x3 -> x0, local copies, waits for them, and re-layouts: 7.39 us -> none  [the longest x2 5.24 us: per_device(): sending = outgoing.reshape(n_col, exp_local, capacity, n_dp, piece)]
  transfers between devices with their start and end apart: 5 -> 0, of which waited for: 4 -> 0; matrix products, arithmetic and copies ran while one was open for 3% -> 0% of each run, Pallas kernels for 0% -> 0%
where the time goes in v1:
time: 82.5 us; the launch traced here: 82 us
  Pallas kernels  74.7 us (91%)
  local copies, waits for them, and re-layouts  5.89 us (7%)
  other arithmetic  1.38 us (2%)
    pallas_call x1, Pallas kernels, fused(): pl.pallas_call(functools.partial(expert_kernel, (tok, cap, piece, units,...  74.7 us
    unnamed x6, local copies, waits for them, and re-layouts  4.64 us

profile of v1, /device:TPU:0, one launch (start us, length us, event | category | flops | bytes accessed | tf_op | source)
XLA Modules:
  0.0 82.0 jit_solution(16215972543672062662)
XLA Ops:
  0.0 0.7 convert_bitcast_fusion
  0.7 0.1 copy.19
  0.8 0.7 reduce_precision.3
  1.4 0.1 copy.16
  1.5 0.8 copy.15
  2.3 0.8 copy.17
  3.1 0.9 %fusion = (bf16[16,2048]{1,0:T(8,128)(2,1)S(1)}, bf16[16,2048]{1,0:T(8,128)(2,1)S(1)}) fusion(bf16[16,4096]{1,0:T(8,128)(2,1)} %param.8), kind=kLoop, calls=%fused_computation.4 | loop fusion | bytes 262144 | tf_op jit(solution)/shard_map/slice | solution.py:334
  3.9 0.1 concatenate.10
  4.0 0.1 concatenate.11
  4.2 1.5 %copy.21.a_in_hbm = bf16[2,2048,64]{2,1,0:T(8,128)(2,1)S(1)} copy(bf16[2,2048,64]{1,2,0:T(8,128)(2,1)} %param.14) | data formatting | bytes 1048576 | tf_op args[6]
  5.7 0.0 copy-start
  5.7 0.9 %copy-done = bf16[2,64,1024]{2,1,0:T(8,128)(2,1)S(1)} copy-done((bf16[2,64,1024]{2,1,0:T(8,128)(2,1)S(1)}, bf16[2,64,1024]{2,1,0:T(8,128)(2,1)}, u32[]{:S(2)}) %copy-start) | copy-done | bytes 262168
  6.6 74.7 %shard_map.82 = bf16[16,4096]{1,0:T(8,128)(2,1)S(1)} custom-call(bf16[2,16,2176]{2,1,0:T(8,128)(2,1)S(1)} %pad_maximum_fusion.xe, bf16[2,2048,1024]{2,1,0:T(8,128)(2,1)} %w_up_hbm.1, bf16[2,1024,2048]{2,1,0:T(8,128)(2,1)} %w_down_hbm.1, bf16[2,2048,64]{2,1,0:T(8,128)(2,1)S(1)} %copy.21.a_in_hbm, bf16[2,64,1024]{2,1,0:T(8,128)(2,1)S(1)} %copy-done), custom_call_target="tpu_custom_call" | custom-call | tf_op jit(solution)/shard_map/pallas_call | solution.py:346
  81.4 0.7 copy.23
  (4 shorter events, 0.0 us)
Async XLA Ops:
  5.7 1.0 %copy-start = (bf16[2,64,1024]{2,1,0:T(8,128)(2,1)S(1)}, bf16[2,64,1024]{2,1,0:T(8,128)(2,1)}, u32[]{:S(2)}) copy-start(bf16[2,64,1024]{2,1,0:T(8,128)(2,1)} %a_out_hbm.1) | copy-start | bytes 786436

commit v2 on v0

--- a/solution.py
+++ b/solution.py
@@ -1,9 +1,427 @@
+import functools
+
 import jax
 import jax.numpy as jnp
 from jax import lax
+from jax.experimental import pallas as pl
+from jax.experimental.pallas import tpu as pltpu
 from jax.sharding import PartitionSpec as P
 
 RANK = 16
+MESH = pl.DeviceIdType.MESH
+BF = jnp.bfloat16
+F32 = jnp.float32
+LANES = 128
+NZ = 4
+
+
+def equal_iota(shape):
+    same = lax.broadcasted_iota(jnp.int32, shape, 0) == lax.broadcasted_iota(jnp.int32, shape, 1)
+    return jnp.where(same, 1.0, 0.0)
+
+
+def expert_kernel(
+    dims,
+    tokens,
+    routes_t,
+    gates_t,
+    tenants_t,
+    w_up_hbm,
+    w_down_hbm,
+    a_in_hbm,
+    a_out_hbm,
+    out,
+    w_up,
+    w_down,
+    a_in,
+    a_out,
+    first_out,
+    grid,
+    packed,
+    pick,
+    part,
+    peer,
+    rows_out,
+    y_part,
+    core_in,
+    y_send,
+    y_in,
+    z_send,
+    z_in,
+    x_send,
+    x_in,
+    load_sem,
+    tx_s,
+    tx_r,
+    ty_s,
+    ty_r,
+    tz_s,
+    tz_r,
+    tc_s,
+    tc_r,
+    v_s,
+    v_r,
+    c_s,
+    c_r,
+    y_s,
+    y_r,
+    z_s,
+    z_r,
+    x_s,
+    x_r,
+):
+    tok, cap, piece, units, cols = dims
+    unit = 2 * tok
+    chunk = 4 * unit
+    rows = (chunk // tok) * cap
+    x = lax.axis_index("dp")
+    e = lax.axis_index("expert")
+    z = e // 4
+    y = (e // 2) % 2
+    c = e % 2
+    x_dev = (1 - x, e)
+    y_dev = (x, z * 4 + (1 - y) * 2 + c)
+    c_dev = (x, z * 4 + y * 2 + (1 - c))
+    z_of = {1: z + 1 - 2 * (z % 2), 2: (z + 2) % 4, 3: 3 - z}
+    z_dev = {q: (x, z_of[q] * 4 + y * 2 + c) for q in z_of}
+
+    def place(core, row):
+        return pl.ds(pl.multiple_of((core * 2 + row) * unit, unit), unit)
+
+    def remote(src, dst, ss, rs, dev):
+        return pltpu.make_async_remote_copy(
+            src_ref=src, dst_ref=dst, send_sem=ss, recv_sem=rs, device_id=dev, device_id_type=MESH
+        )
+
+    loads = [
+        pltpu.make_async_copy(w_up_hbm, w_up, load_sem.at[0]),
+        pltpu.make_async_copy(a_in_hbm, a_in, load_sem.at[1]),
+        pltpu.make_async_copy(a_out_hbm, a_out, load_sem.at[2]),
+        pltpu.make_async_copy(w_down_hbm, w_down, load_sem.at[3]),
+    ]
+    for copy in loads:
+        copy.start()
+
+    barrier = pltpu.get_barrier_semaphore()
+    for dev in [x_dev, y_dev, c_dev] + [z_dev[q] for q in z_of]:
+        pl.semaphore_signal(barrier, inc=1, device_id=dev, device_id_type=MESH)
+
+    gates = gates_t[...]
+    high = gates.astype(BF).astype(F32)
+    stacked = jnp.concatenate(
+        [
+            routes_t[...].astype(F32),
+            high,
+            gates - high,
+            jnp.broadcast_to(tenants_t[...].astype(F32), (8, tok)),
+        ],
+        axis=0,
+    )
+    meta = lax.dot_general(
+        stacked, equal_iota((32, LANES)), (((0,), (0,)), ((), ())), preferred_element_type=F32
+    ).astype(BF)
+
+    def half(dp):
+        return pl.ds(pl.multiple_of((c * 2 + y) * unit + dp * tok, tok), tok)
+
+    first_out[:, 0:piece] = tokens[:, pl.ds(pl.multiple_of((1 - x) * piece, piece), piece)]
+    first_out[:, piece:] = meta
+    grid[0, half(x), 0:piece] = tokens[:, pl.ds(pl.multiple_of(x * piece, piece), piece)]
+    grid[0, half(x), piece:] = meta
+    pl.semaphore_wait(barrier, 3 + NZ - 1)
+
+    sends = []
+
+    def go(*args):
+        cp = remote(*args)
+        cp.start()
+        sends.append(cp)
+        return cp
+
+    go(first_out, grid.at[0, half(x)], tx_s, tx_r, x_dev)
+    remote(first_out, grid.at[0, half(1 - x)], tx_s, tx_r, x_dev).wait_recv()
+
+    own = place(c, y)
+    over = place(c, 1 - y)
+
+    def send_y(q):
+        go(grid.at[q, own], grid.at[q, own], ty_s.at[q], ty_r.at[q], y_dev)
+
+    def wait_y(q):
+        remote(grid.at[q, over], grid.at[q, over], ty_s.at[q], ty_r.at[q], y_dev).wait_recv()
+
+    def send_z(q):
+        go(grid.at[0, own], grid.at[q, own], tz_s.at[q], tz_r.at[q], z_dev[q])
+
+    def wait_z(q):
+        remote(grid.at[q, own], grid.at[q, own], tz_s.at[q], tz_r.at[q], z_dev[q]).wait_recv()
+
+    def send_c(q, which):
+        spot = own if which == 0 else over
+        go(grid.at[q, spot], grid.at[q, spot], tc_s.at[q, which], tc_r.at[q, which], c_dev)
+
+    def wait_c(q):
+        for which, row in ((0, y), (1, 1 - y)):
+            spot = place(1 - c, row)
+            remote(
+                grid.at[q, spot], grid.at[q, spot], tc_s.at[q, which], tc_r.at[q, which], c_dev
+            ).wait_recv()
+
+    def arrive_z(q):
+        wait_z(q)
+        send_y(q)
+        send_c(q, 0)
+
+    def arrive_y(q):
+        wait_y(q)
+        send_c(q, 1)
+
+    def compact(q):
+        wait_c(q)
+        flat = lax.dot_general(
+            equal_iota((LANES, LANES)).astype(BF),
+            grid[q, :, piece:],
+            (((1,), (1,)), ((), ())),
+            preferred_element_type=F32,
+        )
+        t0 = lax.broadcasted_iota(jnp.int32, (chunk, chunk), 0)
+        t1 = lax.broadcasted_iota(jnp.int32, (chunk, chunk), 1)
+        before = jnp.where((t0 // tok == t1 // tok) & (t0 < t1), 1.0, 0.0).astype(BF)
+        r0 = lax.broadcasted_iota(jnp.int32, (rows, chunk), 0)
+        r1 = lax.broadcasted_iota(jnp.int32, (rows, chunk), 1)
+        same = r0 // cap == r1 // tok
+        slot = (r0 % cap).astype(F32)
+        for j in range(2):
+            expert = (2 * e + j).astype(F32)
+            named = jnp.sum(jnp.where(flat[0:8] == expert, 1.0, 0.0), axis=0, keepdims=True)
+            named = jnp.broadcast_to(named, (16, chunk))
+            rank = jnp.dot(named.astype(BF), before, preferred_element_type=F32)
+            hit = same & (slot == rank[0:1]) & (named[0:1] > 0.5)
+            pick[q, j * rows : (j + 1) * rows, :] = jnp.where(hit, 1.0, 0.0).astype(BF)
+        packed[q, :, piece:] = jnp.dot(
+            pick[q], grid[q, :, piece:], preferred_element_type=F32
+        ).astype(BF)
+        step = 512
+
+        def body(n, carry):
+            at = pl.ds(pl.multiple_of(n * step, step), step)
+            packed[q, :, at] = jnp.dot(
+                pick[q], grid[q, :, at], preferred_element_type=F32
+            ).astype(BF)
+            return carry
+
+        lax.fori_loop(0, piece // step, body, 0)
+
+    values = {}
+
+    def up(q):
+        compact(q)
+        if q == 0:
+            loads[0].wait()
+            loads[1].wait()
+            loads[2].wait()
+        for j in range(2):
+            here = pl.ds(j * rows, rows)
+            low = lax.dot_general(
+                packed[q, here, 0:piece],
+                a_in[j],
+                (((1,), (1,)), ((), ())),
+                preferred_element_type=F32,
+            )
+            tenant = packed[q, here, piece + 24 : piece + 25].astype(F32)
+            owner = (lax.broadcasted_iota(jnp.int32, (rows, cols), 1) // RANK).astype(F32)
+            low = jnp.where(owner == tenant, low, 0.0).astype(BF)
+            step = 512
+
+            def body(n, carry):
+                at = pl.ds(pl.multiple_of(n * step, step), step)
+                value = jnp.dot(
+                    packed[q, here, 0:piece], w_up[j, :, at], preferred_element_type=F32
+                )
+                value = value + jnp.dot(low, a_out[j, :, at], preferred_element_type=F32)
+                part[q, j, :, at] = value.astype(BF)
+                return carry
+
+            lax.fori_loop(0, units // step, body, 0)
+            values[q, j] = go(part.at[q, j], peer.at[q, j], v_s.at[q, j], v_r.at[q, j], x_dev)
+
+    mine = pl.ds(pl.multiple_of(c * 2 * unit, 2 * unit), 2 * unit)
+    theirs = pl.ds(pl.multiple_of((1 - c) * 2 * unit, 2 * unit), 2 * unit)
+    cores, rights, lines = {}, {}, {}
+
+    def down(q):
+        for j in range(2):
+            values[q, j].wait_recv()
+            here = pl.ds(j * rows, rows)
+            info = packed[q, here, piece:].astype(F32)
+            expert = (2 * e + j).astype(F32)
+            gate = jnp.where(info[:, 0:8] == expert, info[:, 8:16] + info[:, 16:24], 0.0)
+            gate = jnp.sum(gate, axis=1, keepdims=True)
+            value = part[q, j].astype(F32) + peer[q, j].astype(F32)
+            hidden = (value / (1.0 + jnp.exp(-value))).astype(BF)
+            step = 512
+
+            def body(n, carry):
+                at = pl.ds(pl.multiple_of(n * step, step), step)
+                value = jnp.dot(hidden, w_down[j, :, at], preferred_element_type=F32)
+                rows_out[here, at] = (value * gate).astype(BF)
+                return carry
+
+            lax.fori_loop(0, piece // step, body, 0)
+        back = lax.dot_general(
+            equal_iota((chunk, chunk)).astype(BF),
+            pick[q],
+            (((1,), (1,)), ((), ())),
+            preferred_element_type=F32,
+        ).astype(BF)
+
+        def body(n, carry):
+            at = pl.ds(pl.multiple_of(n * step, step), step)
+            y_part[q, :, at] = jnp.dot(
+                back, rows_out[:, at], preferred_element_type=F32
+            ).astype(BF)
+            return carry
+
+        lax.fori_loop(0, piece // step, body, 0)
+        cores[q] = go(y_part.at[q, theirs], core_in.at[q], c_s.at[q], c_r.at[q], c_dev)
+
+    def spot(row):
+        return pl.ds(pl.multiple_of(row * unit, unit), unit)
+
+    def add_core(q):
+        cores[q].wait_recv()
+        y_send[q] = (
+            y_part[q, place(c, 1 - y)].astype(F32) + core_in[q, spot(1 - y)].astype(F32)
+        ).astype(BF)
+        rights[q] = go(y_send.at[q], y_in.at[q], y_s.at[q], y_r.at[q], y_dev)
+
+    def add_y(q):
+        rights[q].wait_recv()
+        z_send[q] = (
+            y_part[q, place(c, y)].astype(F32)
+            + core_in[q, spot(y)].astype(F32)
+            + y_in[q].astype(F32)
+        ).astype(BF)
+        if q:
+            lines[q] = go(z_send.at[q], z_in.at[q], z_s.at[q], z_r.at[q], z_dev[q])
+
+    send_z(3)
+    send_y(0)
+    send_c(0, 0)
+    send_z(1)
+    send_z(2)
+    arrive_y(0)
+    up(0)
+    arrive_z(3)
+    arrive_z(1)
+    arrive_y(3)
+    up(3)
+    arrive_z(2)
+    arrive_y(1)
+    loads[3].wait()
+    down(0)
+    arrive_y(2)
+    up(2)
+    add_core(0)
+    down(3)
+    add_y(0)
+    up(1)
+    add_core(3)
+    down(2)
+    add_y(3)
+    add_core(2)
+    down(1)
+    add_core(1)
+    add_y(2)
+    add_y(1)
+    total = z_send[0].astype(F32)
+    for q in (3, 2, 1):
+        lines[q].wait_recv()
+        total = total + z_in[q].astype(F32)
+    x_send[...] = total.astype(BF).reshape(2, tok, piece)
+    last = go(x_send.at[1 - x], x_in, x_s, x_r, x_dev)
+    out[:, pl.ds(pl.multiple_of(x * piece, piece), piece)] = x_send[x]
+    last.wait_recv()
+    out[:, pl.ds(pl.multiple_of((1 - x) * piece, piece), piece)] = x_in[...]
+    for cp in sends:
+        cp.wait_send()
+
+
+def fused(
+    tokens, route_ids, gate_weights, tenant_ids, up_weight, down_weight, adapter_in, adapter_out
+):
+    tok = tokens.shape[0]
+    piece = up_weight.shape[1]
+    units = up_weight.shape[2]
+    cols = adapter_in.shape[2]
+    experts_all = up_weight.shape[0] * lax.axis_size("expert")
+    cap = max(2, 2 * tok * route_ids.shape[1] // experts_all)
+    a_in_t = jnp.swapaxes(adapter_in, 1, 2)
+    unit = 2 * tok
+    chunk = 4 * unit
+    rows = (chunk // tok) * cap
+    dma = pltpu.SemaphoreType.DMA
+    vm = lambda *shape: pltpu.VMEM(shape, BF)
+    any_spec = pl.BlockSpec(memory_space=pl.ANY)
+    vmem_spec = pl.BlockSpec(memory_space=pltpu.VMEM)
+    return pl.pallas_call(
+        functools.partial(expert_kernel, (tok, cap, piece, units, cols)),
+        out_shape=jax.ShapeDtypeStruct(tokens.shape, BF),
+        in_specs=[vmem_spec] * 4 + [any_spec] * 4,
+        out_specs=vmem_spec,
+        scratch_shapes=[
+            vm(*up_weight.shape),
+            vm(*down_weight.shape),
+            vm(*a_in_t.shape),
+            vm(*adapter_out.shape),
+            vm(tok, piece + LANES),
+            vm(NZ, chunk, piece + LANES),
+            vm(NZ, 2 * rows, piece + LANES),
+            vm(NZ, 2 * rows, chunk),
+            vm(NZ, 2, rows, units),
+            vm(NZ, 2, rows, units),
+            vm(2 * rows, piece),
+            vm(NZ, chunk, piece),
+            vm(NZ, 2 * unit, piece),
+            vm(NZ, unit, piece),
+            vm(NZ, unit, piece),
+            vm(NZ, unit, piece),
+            vm(NZ, unit, piece),
+            vm(2, tok, piece),
+            vm(tok, piece),
+            dma((4,)),
+            dma,
+            dma,
+            dma((NZ,)),
+            dma((NZ,)),
+            dma((NZ,)),
+            dma((NZ,)),
+            dma((NZ, 2)),
+            dma((NZ, 2)),
+            dma((NZ, 2)),
+            dma((NZ, 2)),
+            dma((NZ,)),
+            dma((NZ,)),
+            dma((NZ,)),
+            dma((NZ,)),
+            dma((NZ,)),
+            dma((NZ,)),
+            dma,
+            dma,
+        ],
+        compiler_params=pltpu.CompilerParams(
+            collective_id=0, has_side_effects=True, vmem_limit_bytes=48 * 1024 * 1024
+        ),
+    )(
+        tokens,
+        route_ids.T,
+        gate_weights.T,
+        tenant_ids.reshape(1, tok),
+        up_weight,
+        down_weight,
+        a_in_t,
+        adapter_out,
+    )
 
 
 def per_device(
@@ -105,6 +523,7 @@
         P("expert", "dp", None),
         P("expert", None, None),
     )
+    small = mesh.shape["dp"] == 2 and mesh.shape["expert"] == 4 * NZ
     return jax.shard_map(
-        per_device, mesh=mesh, in_specs=placed, out_specs=P(("dp", "expert"), None), check_vma=False
-    )
+        fused if small else per_device, mesh=mesh, in_specs=placed, out_specs=P(("dp", "expert"), None), check_vma=False
+    )

time: 278 us -> 75.1 us (0.27)
  blocking collectives: 141 us -> 0 us
  waiting for transfers between devices: 69.9 us -> 0 us
  Pallas kernels: 0 us -> 69.3 us
  local copies, waits for them, and re-layouts: 23 us -> 5.58 us
  matrix products: 16.9 us -> 0 us
  between operations: 13.3 us -> 0.02 us
  starting transfers between devices: 9.27 us -> 0 us
  other arithmetic: 3.64 us -> 0 us
    all_to_all x4 -> x0, blocking collectives: 141 us -> none  [the longest x1 53.3 us: per_device(): lax.all_to_all(lax.all_to_all(sending, 'dp', split_axis=3, concat_axis=2,...]
    pallas_call x0 -> x1, Pallas kernels: none -> 69.3 us  [fused(): pl.pallas_call(functools.partial(expert_kernel, (tok, cap, piece, units,...]
    all_to_all x2 -> x0, waiting for transfers between devices: 32.1 us -> none  [the longest x1 25.9 us: per_device(): lax.all_to_all(lax.all_to_all(going_back, 'expert', split_axis=2, concat_...]
    all_gather x1 -> x0, waiting for transfers between devices: 21.5 us -> none  [per_device(): lax.all_gather(hidden_portion, 'dp', axis=2, tiled=True)]
    dot_general x4 -> x0, matrix products: 16.9 us -> none  [the longest x1 6.72 us: per_device(): jnp.einsum('erd,edf->erf', grid, up_weight, preferred_element_type=jnp.fl...]
    reduce_scatter x1 -> x0, waiting for transfers between devices: 16.3 us -> none  [per_device(): lax.psum_scatter(up_part.astype(jnp.bfloat16), 'dp', scatter_dimension=2,...]
    all_to_all x2 -> x0, starting transfers between devices: 9 us -> none  [the longest x1 5.11 us: per_device(): lax.all_to_all(lax.all_to_all(tag_send, 'dp', split_axis=3, concat_axis=2...]
    reshape x3 -> x0, local copies, waits for them, and re-layouts: 7.39 us -> none  [the longest x2 5.24 us: per_device(): sending = outgoing.reshape(n_col, exp_local, capacity, n_dp, piece)]
  transfers between devices with their start and end apart: 5 -> 0, of which waited for: 4 -> 0; matrix products, arithmetic and copies ran while one was open for 3% -> 0% of each run, Pallas kernels for 0% -> 0%
where the time goes in v2:
time: 75.1 us; the launch traced here: 74.9 us
  Pallas kernels  69.3 us (92%)
  local copies, waits for them, and re-layouts  5.58 us (7%)
    pallas_call x1, Pallas kernels, fused(): pl.pallas_call(functools.partial(expert_kernel, (tok, cap, piece, units,...  69.3 us
    unnamed x13, local copies, waits for them, and re-layouts  5.58 us

profile of v2, /device:TPU:0, one launch (start us, length us, event | category | flops | bytes accessed | tf_op | source)
XLA Modules:
  0.0 74.9 jit_solution(7657754531441383166)
XLA Ops:
  0.0 0.0 copy-start
  0.0 1.0 %copy-done = bf16[2,2048,64]{1,2,0:T(8,128)(2,1)S(1)} copy-done((bf16[2,2048,64]{1,2,0:T(8,128)(2,1)S(1)}, bf16[2,2048,64]{1,2,0:T(8,128)(2,1)}, u32[]{:S(2)}) %copy-start) | copy-done | bytes 524312
  1.0 0.0 copy-start.1
  1.0 0.9 %copy-done.1 = bf16[2,64,1024]{2,1,0:T(8,128)(2,1)S(1)} copy-done((bf16[2,64,1024]{2,1,0:T(8,128)(2,1)S(1)}, bf16[2,64,1024]{2,1,0:T(8,128)(2,1)}, u32[]{:S(2)}) %copy-start.1) | copy-done | bytes 262168
  2.0 0.0 copy-start.2
  2.0 0.9 %copy-done.2 = bf16[16,4096]{1,0:T(8,128)(2,1)S(1)} copy-done((bf16[16,4096]{1,0:T(8,128)(2,1)S(1)}, bf16[16,4096]{1,0:T(8,128)(2,1)}, u32[]{:S(2)}) %copy-start.2) | copy-done | bytes 131096
  2.9 0.0 copy-start.3
  2.9 0.7 copy-done.3
  3.6 0.0 copy-start.4
  3.6 0.7 copy-done.4
  4.3 0.0 copy-start.5
  4.3 0.7 copy-done.5
  4.9 69.3 %shard_map.82 = bf16[16,4096]{1,0:T(8,128)(2,1)S(1)} custom-call(bf16[16,4096]{1,0:T(8,128)(2,1)S(1)} %copy-done.2, s32[8,16]{1,0:T(8,128)S(1)} %bitcast.5, f32[8,16]{1,0:T(8,128)S(1)} %bitcast.6, s32[1,16]{1,0:T(1,128)S(1)} %bitcast.7, bf16[2,2048,1024]{2,1,0:T(8,128)(2,1)} %w_up_hbm.1, bf16[2,1024,2048]{2,1,0:T(8,128)(2,1)} %w_down_hbm.1, ...), custom_call_target="tpu_custom_call" | custom-call | tf_op jit(solution)/shard_map/pallas_call | solution.py:367
  74.2 0.7 copy.10
Async XLA Ops:
  0.0 1.0 %copy-start = (bf16[2,2048,64]{1,2,0:T(8,128)(2,1)S(1)}, bf16[2,2048,64]{1,2,0:T(8,128)(2,1)}, u32[]{:S(2)}) copy-start(bf16[2,2048,64]{1,2,0:T(8,128)(2,1)} %param.14) | copy-start | bytes 1572868
  1.0 0.9 %copy-start.1 = (bf16[2,64,1024]{2,1,0:T(8,128)(2,1)S(1)}, bf16[2,64,1024]{2,1,0:T(8,128)(2,1)}, u32[]{:S(2)}) copy-start(bf16[2,64,1024]{2,1,0:T(8,128)(2,1)} %a_out_hbm.1) | copy-start | bytes 786436
  2.0 0.9 %copy-start.2 = (bf16[16,4096]{1,0:T(8,128)(2,1)S(1)}, bf16[16,4096]{1,0:T(8,128)(2,1)}, u32[]{:S(2)}) copy-start(bf16[16,4096]{1,0:T(8,128)(2,1)} %tokens.1) | copy-start | bytes 393220
  2.9 0.7 copy-start.3
  3.6 0.7 copy-start.4
  4.3 0.7 copy-start.5

commit v3 on v2

v3 whole, which is shorter than its diff:
```python
import functools

import jax
import jax.numpy as jnp
from jax import lax
from jax.experimental import pallas as pl
from jax.experimental.pallas import tpu as pltpu
from jax.sharding import PartitionSpec as P

RANK = 16
MESH = pl.DeviceIdType.MESH
BF = jnp.bfloat16
F32 = jnp.float32
LANES = 128
NZ = 4


def equal_iota(shape):
    same = lax.broadcasted_iota(jnp.int32, shape, 0) == lax.broadcasted_iota(jnp.int32, shape, 1)
    return jnp.where(same, 1.0, 0.0)


def expert_kernel(
    dims,
    tokens_hbm,
    routes_hbm,
    gates_hbm,
    tenants_hbm,
    w_up_hbm,
    w_down_hbm,
    a_in_hbm,
    a_out_hbm,
    out,
    tokens,
    routes_t,
    gates_t,
    tenants_t,
    w_up,
    w_down,
    a_in,
    a_out,
    first_out,
    grid,
    packed,
    pick,
    part,
    peer,
    rows_out,
    y_part,
    core_in,
    y_send,
    y_in,
    z_send,
    z_in,
    x_send,
    x_in,
    load_sem,
    tx_s,
    tx_r,
    ty_s,
    ty_r,
    tz_s,
    tz_r,
    tc_s,
    tc_r,
    v_s,
    v_r,
    c_s,
    c_r,
    y_s,
    y_r,
    z_s,
    z_r,
    x_s,
    x_r,
):
    tok, cap, piece, units, cols = dims
    unit = 2 * tok
    size = 2 * unit
    rows = (size // tok) * cap
    x = lax.axis_index("dp")
    e = lax.axis_index("expert")
    z = e // 4
    y = (e // 2) % 2
    c = e % 2
    x_dev = (1 - x, e)
    y_dev = (x, z * 4 + (1 - y) * 2 + c)
    c_dev = (x, z * 4 + y * 2 + (1 - c))
    z_of = {1: z + 1 - 2 * (z % 2), 2: (z + 2) % 4, 3: 3 - z}
    z_dev = {q: (x, z_of[q] * 4 + y * 2 + c) for q in z_of}
    mine = pl.ds(pl.multiple_of(c * unit, unit), unit)
    theirs = pl.ds(pl.multiple_of((1 - c) * unit, unit), unit)

    def remote(src, dst, ss, rs, dev):
        return pltpu.make_async_remote_copy(
            src_ref=src, dst_ref=dst, send_sem=ss, recv_sem=rs, device_id=dev, device_id_type=MESH
        )

    pairs = [
        (tokens_hbm, tokens),
        (routes_hbm, routes_t),
        (gates_hbm, gates_t),
        (tenants_hbm, tenants_t),
        (a_in_hbm, a_in),
        (a_out_hbm, a_out),
        (w_up_hbm.at[0], w_up.at[0]),
        (w_up_hbm.at[1], w_up.at[1]),
        (w_down_hbm.at[0], w_down.at[0]),
        (w_down_hbm.at[1], w_down.at[1]),
    ]
    loads = [
        pltpu.make_async_copy(src, dst, load_sem.at[n]) for n, (src, dst) in enumerate(pairs)
    ]
    for copy in loads:
        copy.start()

    barrier = pltpu.get_barrier_semaphore()
    for dev in [x_dev, y_dev, c_dev] + [z_dev[q] for q in z_of]:
        pl.semaphore_signal(barrier, inc=1, device_id=dev, device_id_type=MESH)

    for n in range(4):
        loads[n].wait()
    gates = gates_t[...]
    high = gates.astype(BF).astype(F32)
    stacked = jnp.concatenate(
        [
            routes_t[...].astype(F32),
            high,
            gates - high,
            jnp.broadcast_to(tenants_t[...].astype(F32), (8, tok)),
        ],
        axis=0,
    )
    meta = lax.dot_general(
        stacked, equal_iota((32, LANES)), (((0,), (0,)), ((), ())), preferred_element_type=F32
    ).astype(BF)

    def half(dp):
        return pl.ds(pl.multiple_of(c * unit + dp * tok, tok), tok)

    first_out[:, 0:piece] = tokens[:, pl.ds(pl.multiple_of((1 - x) * piece, piece), piece)]
    first_out[:, piece:] = meta
    grid[0, 0, half(x), 0:piece] = tokens[:, pl.ds(pl.multiple_of(x * piece, piece), piece)]
    grid[0, 0, half(x), piece:] = meta
    pl.semaphore_wait(barrier, 3 + NZ - 1)

    sends = []

    def go(*args):
        cp = remote(*args)
        cp.start()
        sends.append(cp)
        return cp

    go(first_out, grid.at[0, 0, half(x)], tx_s, tx_r, x_dev)

    def send_y(q):
        go(grid.at[q, 0, mine], grid.at[q, 1, mine], ty_s.at[q], ty_r.at[q], y_dev)

    def wait_y(q):
        here = grid.at[q, 1, mine]
        remote(here, here, ty_s.at[q], ty_r.at[q], y_dev).wait_recv()
        send_c(q, 1)

    def send_z(q):
        go(grid.at[0, 0, mine], grid.at[q, 0, mine], tz_s.at[q], tz_r.at[q], z_dev[q])

    def wait_z(q):
        here = grid.at[q, 0, mine]
        remote(here, here, tz_s.at[q], tz_r.at[q], z_dev[q]).wait_recv()
        send_c(q, 0)
        send_y(q)

    def send_c(q, r):
        here = grid.at[q, r, mine]
        go(here, here, tc_s.at[q, r], tc_r.at[q, r], c_dev)

    def compact(q, r):
        here = grid.at[q, r, theirs]
        remote(here, here, tc_s.at[q, r], tc_r.at[q, r], c_dev).wait_recv()
        flat = lax.dot_general(
            equal_iota((LANES, LANES)).astype(BF),
            grid[q, r, :, piece:],
            (((1,), (1,)), ((), ())),
            preferred_element_type=F32,
        )
        t0 = lax.broadcasted_iota(jnp.int32, (size, size), 0)
        t1 = lax.broadcasted_iota(jnp.int32, (size, size), 1)
        before = jnp.where((t0 // tok == t1 // tok) & (t0 < t1), 1.0, 0.0).astype(BF)
        r0 = lax.broadcasted_iota(jnp.int32, (rows, size), 0)
        r1 = lax.broadcasted_iota(jnp.int32, (rows, size), 1)
        same = r0 // cap == r1 // tok
        slot = (r0 % cap).astype(F32)
        for j in range(2):
            expert = (2 * e + j).astype(F32)
            named = jnp.sum(jnp.where(flat[0:8] == expert, 1.0, 0.0), axis=0, keepdims=True)
            named = jnp.broadcast_to(named, (16, size))
            rank = jnp.dot(named.astype(BF), before, preferred_element_type=F32)
            hit = same & (slot == rank[0:1]) & (named[0:1] > 0.5)
            pick[q, r, j * rows : (j + 1) * rows, :] = jnp.where(hit, 1.0, 0.0).astype(BF)

        def put(at):
            value = jnp.dot(
                pick[q, r], grid[q, r, :, at], preferred_element_type=F32
            ).astype(BF)
            for j in range(2):
                packed[q, j, r * rows : (r + 1) * rows, at] = value[j * rows : (j + 1) * rows]

        put(pl.ds(piece, LANES))
        step = 512

        def body(n, carry):
            put(pl.ds(pl.multiple_of(n * step, step), step))
            return carry

        lax.fori_loop(0, piece // step, body, 0)

    values = {}

    def up(q, halves):
        for r in halves:
            compact(q, r)
        here = slice(min(halves) * rows, (max(halves) + 1) * rows)
        many = len(halves) * rows
        for j in range(2):
            if q == 0 and halves == (0,):
                if j == 0:
                    loads[4].wait()
                    loads[5].wait()
                loads[6 + j].wait()
            low = lax.dot_general(
                packed[q, j, here, 0:piece],
                a_in[j],
                (((1,), (1,)), ((), ())),
                preferred_element_type=F32,
            )
            tenant = packed[q, j, here, piece + 24 : piece + 25].astype(F32)
            owner = (lax.broadcasted_iota(jnp.int32, (many, cols), 1) // RANK).astype(F32)
            low = jnp.where(owner == tenant, low, 0.0).astype(BF)
            step = 512

            def body(n, carry):
                at = pl.ds(pl.multiple_of(n * step, step), step)
                value = jnp.dot(
                    packed[q, j, here, 0:piece], w_up[j, :, at], preferred_element_type=F32
                )
                value = value + jnp.dot(low, a_out[j, :, at], preferred_element_type=F32)
                part[q, j, here, at] = value.astype(BF)
                return carry

            lax.fori_loop(0, units // step, body, 0)
        for r in sorted(halves, reverse=q != 0):
            spot = pl.ds(r * rows, rows)
            values[q, r] = go(
                part.at[q, :, spot], peer.at[q, :, spot], v_s.at[q, r], v_r.at[q, r], x_dev
            )

    cores, rights, lines = {}, {}, {}

    def down(q, halves):
        for r in halves:
            values[q, r].wait_recv()
        here = slice(min(halves) * rows, (max(halves) + 1) * rows)
        for j in range(2):
            info = packed[q, j, here, piece:].astype(F32)
            expert = (2 * e + j).astype(F32)
            gate = jnp.where(info[:, 0:8] == expert, info[:, 8:16] + info[:, 16:24], 0.0)
            gate = jnp.sum(gate, axis=1, keepdims=True)
            value = part[q, j, here].astype(F32) + peer[q, j, here].astype(F32)
            hidden = (value / (1.0 + jnp.exp(-value))).astype(BF)
            step = 512

            def body(n, carry):
                at = pl.ds(pl.multiple_of(n * step, step), step)
                value = jnp.dot(hidden, w_down[j, :, at], preferred_element_type=F32)
                value = (value * gate).astype(BF)
                for n_at, r in enumerate(sorted(halves)):
                    rows_out[r, j * rows : (j + 1) * rows, at] = value[
                        n_at * rows : (n_at + 1) * rows
                    ]
                return carry

            lax.fori_loop(0, piece // step, body, 0)
        for r in halves:
            back = lax.dot_general(
                equal_iota((size, size)).astype(BF),
                pick[q, r],
                (((1,), (1,)), ((), ())),
                preferred_element_type=F32,
            ).astype(BF)

            def body(n, carry):
                at = pl.ds(pl.multiple_of(n * step, step), step)
                y_part[q, r, :, at] = jnp.dot(
                    back, rows_out[r, :, at], preferred_element_type=F32
                ).astype(BF)
                return carry

            lax.fori_loop(0, piece // step, body, 0)
            cores[q, r] = go(
                y_part.at[q, r, theirs], core_in.at[q, r], c_s.at[q, r], c_r.at[q, r], c_dev
            )

    def add_core(q):
        cores[q, 1].wait_recv()
        y_send[q] = (y_part[q, 1, mine].astype(F32) + core_in[q, 1].astype(F32)).astype(BF)
        rights[q] = go(y_send.at[q], y_in.at[q], y_s.at[q], y_r.at[q], y_dev)

    wide = piece // 2

    def add_y(q):
        cores[q, 0].wait_recv()
        rights[q].wait_recv()
        for h in range(2):
            at = slice(h * wide, (h + 1) * wide)
            z_send[q, h] = (
                y_part[q, 0, mine, at].astype(F32)
                + core_in[q, 0, :, at].astype(F32)
                + y_in[q, :, at].astype(F32)
            ).astype(BF)
            if q:
                lines[q, h] = go(
                    z_send.at[q, h], z_in.at[q, h], z_s.at[q, h], z_r.at[q, h], z_dev[q]
                )

    remote(first_out, grid.at[0, 0, half(1 - x)], tx_s, tx_r, x_dev).wait_recv()
    send_c(0, 0)
    send_z(3)
    send_y(0)
    send_z(1)
    up(0, (0,))
    wait_z(1)
    wait_y(0)
    up(0, (1,))
    send_z(2)
    wait_z(3)
    up(3, (0,))
    wait_y(1)
    loads[8].wait()
    loads[9].wait()
    down(0, (1, 0))
    wait_y(3)
    up(3, (1,))
    wait_z(2)
    up(2, (0,))
    add_core(0)
    wait_y(2)
    up(2, (1,))
    up(1, (0, 1))
    add_y(0)
    down(3, (1, 0))
    add_core(3)
    down(2, (1, 0))
    add_y(3)
    add_core(2)
    down(1, (1,))
    add_core(1)
    add_y(2)
    down(1, (0,))
    add_y(1)
    lasts = []
    for h in range(2):
        total = z_send[0, h].astype(F32)
        for q in (3, 2, 1):
            lines[q, h].wait_recv()
            total = total + z_in[q, h].astype(F32)
        x_send[h] = total.astype(BF).reshape(2, tok, wide)
        lasts.append(go(x_send.at[h, 1 - x], x_in.at[h], x_s.at[h], x_r.at[h], x_dev))
        out[:, pl.ds(pl.multiple_of(x * piece + h * wide, wide), wide)] = x_send[h, x]
    for h in range(2):
        lasts[h].wait_recv()
        out[:, pl.ds(pl.multiple_of((1 - x) * piece + h * wide, wide), wide)] = x_in[h]
    for cp in sends:
        cp.wait_send()


def fused(
    tokens, route_ids, gate_weights, tenant_ids, up_weight, down_weight, adapter_in, adapter_out
):
    tok = tokens.shape[0]
    piece = up_weight.shape[1]
    units = up_weight.shape[2]
    cols = adapter_in.shape[2]
    experts_all = up_weight.shape[0] * lax.axis_size("expert")
    cap = max(2, 2 * tok * route_ids.shape[1] // experts_all)
    a_in_t = jnp.swapaxes(adapter_in, 1, 2)
    unit = 2 * tok
    size = 2 * unit
    rows = (size // tok) * cap
    dma = pltpu.SemaphoreType.DMA
    vm = lambda *shape: pltpu.VMEM(shape, BF)
    any_spec = pl.BlockSpec(memory_space=pl.ANY)
    vmem_spec = pl.BlockSpec(memory_space=pltpu.VMEM)
    return pl.pallas_call(
        functools.partial(expert_kernel, (tok, cap, piece, units, cols)),
        out_shape=jax.ShapeDtypeStruct(tokens.shape, BF),
        in_specs=[any_spec] * 8,
        out_specs=vmem_spec,
        scratch_shapes=[
            vm(*tokens.shape),
            pltpu.VMEM(route_ids.shape[::-1], jnp.int32),
            pltpu.VMEM(gate_weights.shape[::-1], F32),
            pltpu.VMEM((1, tok), jnp.int32),
            vm(*up_weight.shape),
            vm(*down_weight.shape),
            vm(*a_in_t.shape),
            vm(*adapter_out.shape),
            vm(tok, piece + LANES),
            vm(NZ, 2, size, piece + LANES),
            vm(NZ, 2, 2 * rows, piece + LANES),
            vm(NZ, 2, 2 * rows, size),
            vm(NZ, 2, 2 * rows, units),
            vm(NZ, 2, 2 * rows, units),
            vm(2, 2 * rows, piece),
            vm(NZ, 2, size, piece),
            vm(NZ, 2, unit, piece),
            vm(NZ, unit, piece),
            vm(NZ, unit, piece),
            vm(NZ, 2, unit, piece // 2),
            vm(NZ, 2, unit, piece // 2),
            vm(2, 2, tok, piece // 2),
            vm(2, tok, piece // 2),
            dma((10,)),
            dma,
            dma,
            dma((NZ,)),
            dma((NZ,)),
            dma((NZ,)),
            dma((NZ,)),
            dma((NZ, 2)),
            dma((NZ, 2)),
            dma((NZ, 2)),
            dma((NZ, 2)),
            dma((NZ, 2)),
            dma((NZ, 2)),
            dma((NZ,)),
            dma((NZ,)),
            dma((NZ, 2)),
            dma((NZ, 2)),
            dma((2,)),
            dma((2,)),
        ],
        compiler_params=pltpu.CompilerParams(
            collective_id=0, has_side_effects=True, vmem_limit_bytes=60 * 1024 * 1024
        ),
    )(
        tokens,
        route_ids.T,
        gate_weights.T,
        tenant_ids.reshape(1, tok),
        up_weight,
        down_weight,
        a_in_t,
        adapter_out,
    )


def per_device(
    tokens, route_ids, gate_weights, tenant_ids, up_weight, down_weight, adapter_in, adapter_out
):
    n_dp = lax.axis_size("dp")
    n_col = lax.axis_size("expert")
    tok_count = tokens.shape[0]
    chosen = route_ids.shape[1]
    features = tokens.shape[1]
    exp_local = up_weight.shape[0]
    piece = up_weight.shape[1]
    units = up_weight.shape[2]
    adapter_cols = adapter_in.shape[2]
    experts_all = exp_local * n_col
    capacity = max(2, 2 * tok_count * chosen // experts_all)
    send_rows = experts_all * capacity
    flat_routes = route_ids.reshape(-1)
    order = jnp.arange(flat_routes.shape[0], dtype=jnp.int32)
    same = flat_routes[:, None] == flat_routes[None, :]
    earlier = order[None, :] < order[:, None]
    rank = jnp.sum((same & earlier).astype(jnp.int32), axis=1)
    target = flat_routes * capacity + rank
    outgoing = (
        jnp.zeros((send_rows, features), jnp.bfloat16)
        .at[target]
        .set(jnp.repeat(tokens, chosen, axis=0))
    )
    tag_line = (
        jnp.full((send_rows,), -1.0, jnp.float32)
        .at[target]
        .set(jnp.repeat(tenant_ids, chosen).astype(jnp.float32))
    )
    tag_grid = jnp.broadcast_to(tag_line[:, None], (send_rows, n_dp)).astype(jnp.bfloat16)
    sending = outgoing.reshape(n_col, exp_local, capacity, n_dp, piece)
    tag_send = tag_grid.reshape(n_col, exp_local, capacity, n_dp, 1)
    arrived, arrived_tags = (
        lax.all_to_all(
            lax.all_to_all(sending, "dp", split_axis=3, concat_axis=2, tiled=True),
            "expert",
            split_axis=0,
            concat_axis=2,
            tiled=True,
        ),
        lax.all_to_all(
            lax.all_to_all(tag_send, "dp", split_axis=3, concat_axis=2, tiled=True),
            "expert",
            split_axis=0,
            concat_axis=2,
            tiled=True,
        ),
    )
    rows_all = arrived.shape[2]
    grid = arrived.reshape(exp_local, rows_all, piece)
    tags = arrived_tags.reshape(exp_local, rows_all).astype(jnp.float32)
    up_part = jnp.einsum("erd,edf->erf", grid, up_weight, preferred_element_type=jnp.float32)
    shrink_part = jnp.einsum("erd,edl->erl", grid, adapter_in, preferred_element_type=jnp.float32)
    owner = (jnp.arange(adapter_cols, dtype=jnp.int32) // RANK).astype(jnp.float32)
    shrink = lax.psum(shrink_part.astype(jnp.bfloat16), "dp").astype(jnp.float32)
    keep = owner[None, None, :] == tags[..., None]
    masked_values = jnp.where(keep, shrink, jnp.zeros((), jnp.float32))
    up_portion = lax.psum_scatter(
        up_part.astype(jnp.bfloat16), "dp", scatter_dimension=2, tiled=True
    ).astype(jnp.float32)
    share = units // n_dp
    mapping_portion = lax.dynamic_slice_in_dim(
        adapter_out, lax.axis_index("dp") * share, share, 2
    ).astype(jnp.float32)
    low_rank_adapter = jnp.einsum(
        "erl,elf->erf", masked_values, mapping_portion, precision=lax.Precision.HIGHEST
    )
    hidden_portion = jax.nn.silu(up_portion + low_rank_adapter).astype(jnp.bfloat16)
    hidden_activations = lax.all_gather(hidden_portion, "dp", axis=2, tiled=True)
    expert_out = jnp.einsum(
        "erf,efd->erd", hidden_activations, down_weight, preferred_element_type=jnp.float32
    ).astype(jnp.bfloat16)
    going_back = expert_out.reshape(1, exp_local, rows_all, 1, piece)
    returned = lax.all_to_all(
        lax.all_to_all(going_back, "expert", split_axis=2, concat_axis=0, tiled=True),
        "dp",
        split_axis=2,
        concat_axis=3,
        tiled=True,
    )
    results = returned.reshape(send_rows, features)
    picked = results[target].astype(jnp.float32).reshape(tok_count, chosen, features)
    mixed = jnp.sum(picked * gate_weights[:, :, None], axis=1)
    return mixed.astype(jnp.bfloat16)


def solution(mesh):
    placed = (
        P(("dp", "expert"), None),
        P(("dp", "expert"), None),
        P(("dp", "expert"), None),
        P(("dp", "expert")),
        P("expert", "dp", None),
        P("expert", None, "dp"),
        P("expert", "dp", None),
        P("expert", None, None),
    )
    small = mesh.shape["dp"] == 2 and mesh.shape["expert"] == 4 * NZ
    return jax.shard_map(
        fused if small else per_device, mesh=mesh, in_specs=placed, out_specs=P(("dp", "expert"), None), check_vma=False
    )
```

time: 75.1 us -> 78.5 us (1.045)
  Pallas kernels: 69.3 us -> 76.8 us
  local copies, waits for them, and re-layouts: 5.58 us -> 1.57 us
    pallas_call x1, Pallas kernels: 69.3 us -> 76.8 us  [fused(): pl.pallas_call(functools.partial(expert_kernel, (tok, cap, piece, units,...]
    unnamed x13 -> x1, local copies, waits for them, and re-layouts: 5.58 us -> 1.57 us
where the time goes in v3:
time: 78.5 us; the launch traced here: 78.3 us
  Pallas kernels  76.8 us (98%)
  local copies, waits for them, and re-layouts  1.57 us (2%)
    pallas_call x1, Pallas kernels, fused(): pl.pallas_call(functools.partial(expert_kernel, (tok, cap, piece, units,...  76.8 us

profile of v3, /device:TPU:0, one launch (start us, length us, event | category | flops | bytes accessed | tf_op | source)
XLA Modules:
  0.0 78.3 jit_solution(1637223717879311466)
XLA Ops:
  0.0 76.8 %shard_map.82 = bf16[16,4096]{1,0:T(8,128)(2,1)} custom-call(bf16[16,4096]{1,0:T(8,128)(2,1)} %tokens_hbm.1, s32[8,16]{1,0:T(8,128)} %bitcast.5, f32[8,16]{1,0:T(8,128)} %bitcast.6, s32[1,16]{1,0:T(1,128)} %bitcast.7, bf16[2,2048,1024]{2,1,0:T(8,128)(2,1)} %w_up_hbm.1, bf16[2,1024,2048]{2,1,0:T(8,128)(2,1)} %w_down_hbm.1, bf16[2,64,2048]{2,1,0:T(8,128)(2,1)} %bitcast.4, ...), custom_call_target="tpu_custom_call" | custom-call | tf_op jit(solution)/shard_map/pallas_call | solution.py:394
  76.8 1.6 %copy.10 = bf16[16,4096]{1,0:T(8,128)(2,1)} copy(bf16[16,4096]{1,0:T(8,128)(2,1)} %shard_map.82) | data formatting | bytes 262144

commit v4 on v3

--- a/solution.py
+++ b/solution.py
@@ -13,6 +13,8 @@
 F32 = jnp.float32
 LANES = 128
 NZ = 4
+STEP = 256
+ORDER = (0, 3, 2, 1)
 
 
 def equal_iota(shape):
@@ -77,7 +79,8 @@
     tok, cap, piece, units, cols = dims
     unit = 2 * tok
     size = 2 * unit
-    rows = (size // tok) * cap
+    chunk = 2 * size
+    rows = (chunk // tok) * cap
     x = lax.axis_index("dp")
     e = lax.axis_index("expert")
     z = e // 4
@@ -88,8 +91,6 @@
     c_dev = (x, z * 4 + y * 2 + (1 - c))
     z_of = {1: z + 1 - 2 * (z % 2), 2: (z + 2) % 4, 3: 3 - z}
     z_dev = {q: (x, z_of[q] * 4 + y * 2 + c) for q in z_of}
-    mine = pl.ds(pl.multiple_of(c * unit, unit), unit)
-    theirs = pl.ds(pl.multiple_of((1 - c) * unit, unit), unit)
 
     def remote(src, dst, ss, rs, dev):
         return pltpu.make_async_remote_copy(
@@ -135,13 +136,16 @@
         stacked, equal_iota((32, LANES)), (((0,), (0,)), ((), ())), preferred_element_type=F32
     ).astype(BF)
 
+    def lane(r, core):
+        return pl.ds(pl.multiple_of(r * size + core * unit, unit), unit)
+
     def half(dp):
         return pl.ds(pl.multiple_of(c * unit + dp * tok, tok), tok)
 
     first_out[:, 0:piece] = tokens[:, pl.ds(pl.multiple_of((1 - x) * piece, piece), piece)]
     first_out[:, piece:] = meta
-    grid[0, 0, half(x), 0:piece] = tokens[:, pl.ds(pl.multiple_of(x * piece, piece), piece)]
-    grid[0, 0, half(x), piece:] = meta
+    grid[0, half(x), 0:piece] = tokens[:, pl.ds(pl.multiple_of(x * piece, piece), piece)]
+    grid[0, half(x), piece:] = meta
     pl.semaphore_wait(barrier, 3 + NZ - 1)
 
     sends = []
@@ -152,158 +156,146 @@
         sends.append(cp)
         return cp
 
-    go(first_out, grid.at[0, 0, half(x)], tx_s, tx_r, x_dev)
+    go(first_out, grid.at[0, half(x)], tx_s, tx_r, x_dev)
 
     def send_y(q):
-        go(grid.at[q, 0, mine], grid.at[q, 1, mine], ty_s.at[q], ty_r.at[q], y_dev)
+        go(grid.at[q, lane(0, c)], grid.at[q, lane(1, c)], ty_s.at[q], ty_r.at[q], y_dev)
 
     def wait_y(q):
-        here = grid.at[q, 1, mine]
+        here = grid.at[q, lane(1, c)]
         remote(here, here, ty_s.at[q], ty_r.at[q], y_dev).wait_recv()
         send_c(q, 1)
 
     def send_z(q):
-        go(grid.at[0, 0, mine], grid.at[q, 0, mine], tz_s.at[q], tz_r.at[q], z_dev[q])
+        go(grid.at[0, lane(0, c)], grid.at[q, lane(0, c)], tz_s.at[q], tz_r.at[q], z_dev[q])
 
     def wait_z(q):
-        here = grid.at[q, 0, mine]
+        here = grid.at[q, lane(0, c)]
         remote(here, here, tz_s.at[q], tz_r.at[q], z_dev[q]).wait_recv()
         send_c(q, 0)
         send_y(q)
 
     def send_c(q, r):
-        here = grid.at[q, r, mine]
+        here = grid.at[q, lane(r, c)]
         go(here, here, tc_s.at[q, r], tc_r.at[q, r], c_dev)
 
-    def compact(q, r):
-        here = grid.at[q, r, theirs]
-        remote(here, here, tc_s.at[q, r], tc_r.at[q, r], c_dev).wait_recv()
+    def at_place(q):
+        first = ORDER.index(q) * rows
+        return slice(first, first + rows)
+
+    def compact(q):
+        for r in range(2):
+            here = grid.at[q, lane(r, 1 - c)]
+            remote(here, here, tc_s.at[q, r], tc_r.at[q, r], c_dev).wait_recv()
         flat = lax.dot_general(
             equal_iota((LANES, LANES)).astype(BF),
-            grid[q, r, :, piece:],
+            grid[q, :, piece:],
             (((1,), (1,)), ((), ())),
             preferred_element_type=F32,
         )
-        t0 = lax.broadcasted_iota(jnp.int32, (size, size), 0)
-        t1 = lax.broadcasted_iota(jnp.int32, (size, size), 1)
+        t0 = lax.broadcasted_iota(jnp.int32, (chunk, chunk), 0)
+        t1 = lax.broadcasted_iota(jnp.int32, (chunk, chunk), 1)
         before = jnp.where((t0 // tok == t1 // tok) & (t0 < t1), 1.0, 0.0).astype(BF)
-        r0 = lax.broadcasted_iota(jnp.int32, (rows, size), 0)
-        r1 = lax.broadcasted_iota(jnp.int32, (rows, size), 1)
+        r0 = lax.broadcasted_iota(jnp.int32, (rows, chunk), 0)
+        r1 = lax.broadcasted_iota(jnp.int32, (rows, chunk), 1)
         same = r0 // cap == r1 // tok
         slot = (r0 % cap).astype(F32)
         for j in range(2):
             expert = (2 * e + j).astype(F32)
             named = jnp.sum(jnp.where(flat[0:8] == expert, 1.0, 0.0), axis=0, keepdims=True)
-            named = jnp.broadcast_to(named, (16, size))
+            named = jnp.broadcast_to(named, (16, chunk))
             rank = jnp.dot(named.astype(BF), before, preferred_element_type=F32)
             hit = same & (slot == rank[0:1]) & (named[0:1] > 0.5)
-            pick[q, r, j * rows : (j + 1) * rows, :] = jnp.where(hit, 1.0, 0.0).astype(BF)
-
-        def put(at):
-            value = jnp.dot(
-                pick[q, r], grid[q, r, :, at], preferred_element_type=F32
-            ).astype(BF)
+            pick[q, j * rows : (j + 1) * rows, :] = jnp.where(hit, 1.0, 0.0).astype(BF)
+        for n in list(range(0, piece, STEP)) + [piece]:
+            at = slice(n, min(n + STEP, piece + LANES))
+            value = jnp.dot(pick[q], grid[q, :, at], preferred_element_type=F32).astype(BF)
             for j in range(2):
-                packed[q, j, r * rows : (r + 1) * rows, at] = value[j * rows : (j + 1) * rows]
-
-        put(pl.ds(piece, LANES))
-        step = 512
-
-        def body(n, carry):
-            put(pl.ds(pl.multiple_of(n * step, step), step))
-            return carry
-
-        lax.fori_loop(0, piece // step, body, 0)
+                packed[j, at_place(q), at] = value[j * rows : (j + 1) * rows]
 
     values = {}
 
-    def up(q, halves):
-        for r in halves:
-            compact(q, r)
-        here = slice(min(halves) * rows, (max(halves) + 1) * rows)
-        many = len(halves) * rows
+    def span(group):
+        first = ORDER.index(group[0]) * rows
+        return slice(first, first + len(group) * rows)
+
+    def up(*group):
+        for q in group:
+            compact(q)
+        here = span(group)
         for j in range(2):
-            if q == 0 and halves == (0,):
+            if group[0] == 0:
                 if j == 0:
                     loads[4].wait()
                     loads[5].wait()
                 loads[6 + j].wait()
             low = lax.dot_general(
-                packed[q, j, here, 0:piece],
+                packed[j, here, 0:piece],
                 a_in[j],
                 (((1,), (1,)), ((), ())),
                 preferred_element_type=F32,
             )
-            tenant = packed[q, j, here, piece + 24 : piece + 25].astype(F32)
-            owner = (lax.broadcasted_iota(jnp.int32, (many, cols), 1) // RANK).astype(F32)
+            tenant = packed[j, here, piece + 24 : piece + 25].astype(F32)
+            owner = (lax.broadcasted_iota(jnp.int32, low.shape, 1) // RANK).astype(F32)
             low = jnp.where(owner == tenant, low, 0.0).astype(BF)
-            step = 512
-
-            def body(n, carry):
-                at = pl.ds(pl.multiple_of(n * step, step), step)
+            for n in range(0, units, STEP):
+                at = slice(n, n + STEP)
                 value = jnp.dot(
-                    packed[q, j, here, 0:piece], w_up[j, :, at], preferred_element_type=F32
+                    packed[j, here, 0:piece], w_up[j, :, at], preferred_element_type=F32
                 )
                 value = value + jnp.dot(low, a_out[j, :, at], preferred_element_type=F32)
-                part[q, j, here, at] = value.astype(BF)
-                return carry
-
-            lax.fori_loop(0, units // step, body, 0)
-        for r in sorted(halves, reverse=q != 0):
-            spot = pl.ds(r * rows, rows)
-            values[q, r] = go(
-                part.at[q, :, spot], peer.at[q, :, spot], v_s.at[q, r], v_r.at[q, r], x_dev
-            )
+                part[j, here, at] = value.astype(BF)
+            for q in group:
+                spot = at_place(q)
+                values[q, j] = go(
+                    part.at[j, spot], peer.at[j, spot], v_s.at[q, j], v_r.at[q, j], x_dev
+                )
 
     cores, rights, lines = {}, {}, {}
 
-    def down(q, halves):
-        for r in halves:
-            values[q, r].wait_recv()
-        here = slice(min(halves) * rows, (max(halves) + 1) * rows)
+    def down(*group):
+        here = span(group)
         for j in range(2):
-            info = packed[q, j, here, piece:].astype(F32)
+            for q in group:
+                values[q, j].wait_recv()
+            info = packed[j, here, piece:].astype(F32)
             expert = (2 * e + j).astype(F32)
             gate = jnp.where(info[:, 0:8] == expert, info[:, 8:16] + info[:, 16:24], 0.0)
             gate = jnp.sum(gate, axis=1, keepdims=True)
-            value = part[q, j, here].astype(F32) + peer[q, j, here].astype(F32)
+            value = part[j, here].astype(F32) + peer[j, here].astype(F32)
             hidden = (value / (1.0 + jnp.exp(-value))).astype(BF)
-            step = 512
-
-            def body(n, carry):
-                at = pl.ds(pl.multiple_of(n * step, step), step)
+            for n in range(0, piece, STEP):
+                at = slice(n, n + STEP)
                 value = jnp.dot(hidden, w_down[j, :, at], preferred_element_type=F32)
                 value = (value * gate).astype(BF)
-                for n_at, r in enumerate(sorted(halves)):
-                    rows_out[r, j * rows : (j + 1) * rows, at] = value[
+                for n_at, q in enumerate(group):
+                    rows_out[q, j * rows : (j + 1) * rows, at] = value[
                         n_at * rows : (n_at + 1) * rows
                     ]
-                return carry
-
-            lax.fori_loop(0, piece // step, body, 0)
-        for r in halves:
+        for q in group:
             back = lax.dot_general(
-                equal_iota((size, size)).astype(BF),
-                pick[q, r],
+                equal_iota((chunk, chunk)).astype(BF),
+                pick[q],
                 (((1,), (1,)), ((), ())),
                 preferred_element_type=F32,
             ).astype(BF)
-
-            def body(n, carry):
-                at = pl.ds(pl.multiple_of(n * step, step), step)
-                y_part[q, r, :, at] = jnp.dot(
-                    back, rows_out[r, :, at], preferred_element_type=F32
+            for n in range(0, piece, STEP):
+                at = slice(n, n + STEP)
+                y_part[q, :, at] = jnp.dot(
+                    back, rows_out[q, :, at], preferred_element_type=F32
                 ).astype(BF)
-                return carry
-
-            lax.fori_loop(0, piece // step, body, 0)
-            cores[q, r] = go(
-                y_part.at[q, r, theirs], core_in.at[q, r], c_s.at[q, r], c_r.at[q, r], c_dev
-            )
+            for r in (1, 0):
+                cores[q, r] = go(
+                    y_part.at[q, lane(r, 1 - c)],
+                    core_in.at[q, r],
+                    c_s.at[q, r],
+                    c_r.at[q, r],
+                    c_dev,
+                )
 
     def add_core(q):
         cores[q, 1].wait_recv()
-        y_send[q] = (y_part[q, 1, mine].astype(F32) + core_in[q, 1].astype(F32)).astype(BF)
+        y_send[q] = (y_part[q, lane(1, c)].astype(F32) + core_in[q, 1].astype(F32)).astype(BF)
         rights[q] = go(y_send.at[q], y_in.at[q], y_s.at[q], y_r.at[q], y_dev)
 
     wide = piece // 2
@@ -314,7 +306,7 @@
         for h in range(2):
             at = slice(h * wide, (h + 1) * wide)
             z_send[q, h] = (
-                y_part[q, 0, mine, at].astype(F32)
+                y_part[q, lane(0, c), at].astype(F32)
                 + core_in[q, 0, :, at].astype(F32)
                 + y_in[q, :, at].astype(F32)
             ).astype(BF)
@@ -323,40 +315,34 @@
                     z_send.at[q, h], z_in.at[q, h], z_s.at[q, h], z_r.at[q, h], z_dev[q]
                 )
 
-    remote(first_out, grid.at[0, 0, half(1 - x)], tx_s, tx_r, x_dev).wait_recv()
+    remote(first_out, grid.at[0, half(1 - x)], tx_s, tx_r, x_dev).wait_recv()
     send_c(0, 0)
+    send_y(0)
     send_z(3)
-    send_y(0)
     send_z(1)
-    up(0, (0,))
+    wait_y(0)
+    send_z(2)
+    up(0)
+    wait_z(3)
     wait_z(1)
-    wait_y(0)
-    up(0, (1,))
-    send_z(2)
-    wait_z(3)
-    up(3, (0,))
+    wait_y(3)
     wait_y(1)
+    up(3)
+    wait_z(2)
+    wait_y(2)
     loads[8].wait()
     loads[9].wait()
-    down(0, (1, 0))
-    wait_y(3)
-    up(3, (1,))
-    wait_z(2)
-    up(2, (0,))
+    up(2, 1)
+    down(0, 3)
+    add_core(3)
     add_core(0)
-    wait_y(2)
-    up(2, (1,))
-    up(1, (0, 1))
+    add_y(3)
     add_y(0)
-    down(3, (1, 0))
-    add_core(3)
-    down(2, (1, 0))
-    add_y(3)
+    down(2)
     add_core(2)
-    down(1, (1,))
+    down(1)
     add_core(1)
     add_y(2)
-    down(1, (0,))
     add_y(1)
     lasts = []
     for h in range(2):
@@ -386,7 +372,8 @@
     a_in_t = jnp.swapaxes(adapter_in, 1, 2)
     unit = 2 * tok
     size = 2 * unit
-    rows = (size // tok) * cap
+    chunk = 2 * size
+    rows = (chunk // tok) * cap
     dma = pltpu.SemaphoreType.DMA
     vm = lambda *shape: pltpu.VMEM(shape, BF)
     any_spec = pl.BlockSpec(memory_space=pl.ANY)
@@ -406,13 +393,13 @@
             vm(*a_in_t.shape),
             vm(*adapter_out.shape),
             vm(tok, piece + LANES),
-            vm(NZ, 2, size, piece + LANES),
-            vm(NZ, 2, 2 * rows, piece + LANES),
-            vm(NZ, 2, 2 * rows, size),
-            vm(NZ, 2, 2 * rows, units),
-            vm(NZ, 2, 2 * rows, units),
-            vm(2, 2 * rows, piece),
-            vm(NZ, 2, size, piece),
+            vm(NZ, chunk, piece + LANES),
+            vm(2, NZ * rows, piece + LANES),
+            vm(NZ, 2 * rows, chunk),
+            vm(2, NZ * rows, units),
+            vm(2, NZ * rows, units),
+            vm(NZ, 2 * rows, piece),
+            vm(NZ, chunk, piece),
             vm(NZ, 2, unit, piece),
             vm(NZ, unit, piece),
             vm(NZ, unit, piece),

time: 78.5 us -> 68.3 us (0.87)
  Pallas kernels: 76.8 us -> 66.6 us
    pallas_call x1, Pallas kernels: 76.8 us -> 66.6 us  [fused(): pl.pallas_call(functools.partial(expert_kernel, (tok, cap, piece, units,...]
where the time goes in v4:
time: 68.3 us; the launch traced here: 68.2 us
  Pallas kernels  66.6 us (98%)
  local copies, waits for them, and re-layouts  1.57 us (2%)
    pallas_call x1, Pallas kernels, fused(): pl.pallas_call(functools.partial(expert_kernel, (tok, cap, piece, units,...  66.6 us
    unnamed x1, local copies, waits for them, and re-layouts  1.57 us

profile of v4, /device:TPU:0, one launch (start us, length us, event | category | flops | bytes accessed | tf_op | source)
XLA Modules:
  0.0 68.2 jit_solution(7435958237141381255)
XLA Ops:
  0.0 66.6 %shard_map.82 = bf16[16,4096]{1,0:T(8,128)(2,1)} custom-call(bf16[16,4096]{1,0:T(8,128)(2,1)} %tokens_hbm.1, s32[8,16]{1,0:T(8,128)} %bitcast.5, f32[8,16]{1,0:T(8,128)} %bitcast.6, s32[1,16]{1,0:T(1,128)} %bitcast.7, bf16[2,2048,1024]{2,1,0:T(8,128)(2,1)} %w_up_hbm.1, bf16[2,1024,2048]{2,1,0:T(8,128)(2,1)} %w_down_hbm.1, bf16[2,64,2048]{2,1,0:T(8,128)(2,1)} %bitcast.4, ...), custom_call_target="tpu_custom_call" | custom-call | tf_op jit(solution)/shard_map/pallas_call | solution.py:381
  66.6 1.6 %copy.10 = bf16[16,4096]{1,0:T(8,128)(2,1)} copy(bf16[16,4096]{1,0:T(8,128)(2,1)} %shard_map.82) | data formatting | bytes 262144

commit v5 on v4

--- a/solution.py
+++ b/solution.py
@@ -14,7 +14,7 @@
 LANES = 128
 NZ = 4
 STEP = 256
-ORDER = (0, 3, 2, 1)
+ORDER = (0, 2, 3, 1)
 
 
 def equal_iota(shape):
@@ -47,6 +47,7 @@
     pick,
     part,
     peer,
+    active,
     rows_out,
     y_part,
     core_in,
@@ -89,7 +90,7 @@
     x_dev = (1 - x, e)
     y_dev = (x, z * 4 + (1 - y) * 2 + c)
     c_dev = (x, z * 4 + y * 2 + (1 - c))
-    z_of = {1: z + 1 - 2 * (z % 2), 2: (z + 2) % 4, 3: 3 - z}
+    z_of = {1: z + 1 - 2 * (z % 2), 2: (z + 2) % 4}
     z_dev = {q: (x, z_of[q] * 4 + y * 2 + c) for q in z_of}
 
     def remote(src, dst, ss, rs, dev):
@@ -146,7 +147,7 @@
     first_out[:, piece:] = meta
     grid[0, half(x), 0:piece] = tokens[:, pl.ds(pl.multiple_of(x * piece, piece), piece)]
     grid[0, half(x), piece:] = meta
-    pl.semaphore_wait(barrier, 3 + NZ - 1)
+    pl.semaphore_wait(barrier, 5)
 
     sends = []
 
@@ -166,12 +167,15 @@
         remote(here, here, ty_s.at[q], ty_r.at[q], y_dev).wait_recv()
         send_c(q, 1)
 
-    def send_z(q):
-        go(grid.at[0, lane(0, c)], grid.at[q, lane(0, c)], tz_s.at[q], tz_r.at[q], z_dev[q])
+    def send_z(q, dev):
+        src = grid.at[2 if q == 3 else 0, lane(0, c)]
+        go(src, grid.at[q, lane(0, c)], tz_s.at[q], tz_r.at[q], z_dev[dev])
 
     def wait_z(q):
         here = grid.at[q, lane(0, c)]
-        remote(here, here, tz_s.at[q], tz_r.at[q], z_dev[q]).wait_recv()
+        remote(here, here, tz_s.at[q], tz_r.at[q], z_dev[q % 2 or 2]).wait_recv()
+        if q == 2:
+            send_z(3, 1)
         send_c(q, 0)
         send_y(q)
 
@@ -252,94 +256,115 @@
                 )
 
     cores, rights, lines = {}, {}, {}
+    wide = piece // 2
 
     def down(*group):
         here = span(group)
+        gates_of = []
         for j in range(2):
             for q in group:
                 values[q, j].wait_recv()
             info = packed[j, here, piece:].astype(F32)
             expert = (2 * e + j).astype(F32)
             gate = jnp.where(info[:, 0:8] == expert, info[:, 8:16] + info[:, 16:24], 0.0)
-            gate = jnp.sum(gate, axis=1, keepdims=True)
+            gates_of.append(jnp.sum(gate, axis=1, keepdims=True))
             value = part[j, here].astype(F32) + peer[j, here].astype(F32)
-            hidden = (value / (1.0 + jnp.exp(-value))).astype(BF)
-            for n in range(0, piece, STEP):
-                at = slice(n, n + STEP)
-                value = jnp.dot(hidden, w_down[j, :, at], preferred_element_type=F32)
-                value = (value * gate).astype(BF)
-                for n_at, q in enumerate(group):
-                    rows_out[q, j * rows : (j + 1) * rows, at] = value[
-                        n_at * rows : (n_at + 1) * rows
-                    ]
-        for q in group:
-            back = lax.dot_general(
+            active[j, 0 : len(group) * rows] = (value / (1.0 + jnp.exp(-value))).astype(BF)
+        backs = [
+            lax.dot_general(
                 equal_iota((chunk, chunk)).astype(BF),
                 pick[q],
                 (((1,), (1,)), ((), ())),
                 preferred_element_type=F32,
             ).astype(BF)
-            for n in range(0, piece, STEP):
-                at = slice(n, n + STEP)
-                y_part[q, :, at] = jnp.dot(
-                    back, rows_out[q, :, at], preferred_element_type=F32
-                ).astype(BF)
-            for r in (1, 0):
-                cores[q, r] = go(
-                    y_part.at[q, lane(r, 1 - c)],
-                    core_in.at[q, r],
-                    c_s.at[q, r],
-                    c_r.at[q, r],
-                    c_dev,
-                )
+            for q in group
+        ]
+        for h in range(2):
+            for n in range(0, wide, STEP):
+                full = slice(h * wide + n, h * wide + n + STEP)
+                for j in range(2):
+                    value = jnp.dot(
+                        active[j, 0 : len(group) * rows],
+                        w_down[j, :, full],
+                        preferred_element_type=F32,
+                    )
+                    value = (value * gates_of[j]).astype(BF)
+                    for n_at, q in enumerate(group):
+                        rows_out[q, j * rows : (j + 1) * rows, full] = value[
+                            n_at * rows : (n_at + 1) * rows
+                        ]
+            for q, back in zip(group, backs):
+                for n in range(0, wide, STEP):
+                    full = slice(h * wide + n, h * wide + n + STEP)
+                    y_part[q, h, :, n : n + STEP] = jnp.dot(
+                        back, rows_out[q, :, full], preferred_element_type=F32
+                    ).astype(BF)
+                for r in (1, 0):
+                    cores[q, h, r] = go(
+                        y_part.at[q, h, lane(r, 1 - c)],
+                        core_in.at[q, h, r],
+                        c_s.at[q, h, r],
+                        c_r.at[q, h, r],
+                        c_dev,
+                    )
 
     def add_core(q):
-        cores[q, 1].wait_recv()
-        y_send[q] = (y_part[q, lane(1, c)].astype(F32) + core_in[q, 1].astype(F32)).astype(BF)
-        rights[q] = go(y_send.at[q], y_in.at[q], y_s.at[q], y_r.at[q], y_dev)
-
-    wide = piece // 2
+        for h in range(2):
+            cores[q, h, 1].wait_recv()
+            y_send[q, h] = (
+                y_part[q, h, lane(1, c)].astype(F32) + core_in[q, h, 1].astype(F32)
+            ).astype(BF)
+            rights[q, h] = go(
+                y_send.at[q, h], y_in.at[q, h], y_s.at[q, h], y_r.at[q, h], y_dev
+            )
 
     def add_y(q):
-        cores[q, 0].wait_recv()
-        rights[q].wait_recv()
         for h in range(2):
-            at = slice(h * wide, (h + 1) * wide)
-            z_send[q, h] = (
-                y_part[q, lane(0, c), at].astype(F32)
-                + core_in[q, 0, :, at].astype(F32)
-                + y_in[q, :, at].astype(F32)
-            ).astype(BF)
+            cores[q, h, 0].wait_recv()
+            rights[q, h].wait_recv()
+            value = (
+                y_part[q, h, lane(0, c)].astype(F32)
+                + core_in[q, h, 0].astype(F32)
+                + y_in[q, h].astype(F32)
+            )
+            if q == 2:
+                lines[3, h].wait_recv()
+                value = value + z_in[3, h].astype(F32)
+            z_send[q, h] = value.astype(BF)
             if q:
                 lines[q, h] = go(
-                    z_send.at[q, h], z_in.at[q, h], z_s.at[q, h], z_r.at[q, h], z_dev[q]
+                    z_send.at[q, h],
+                    z_in.at[q, h],
+                    z_s.at[q, h],
+                    z_r.at[q, h],
+                    z_dev[2 if q == 2 else 1],
                 )
 
     remote(first_out, grid.at[0, half(1 - x)], tx_s, tx_r, x_dev).wait_recv()
     send_c(0, 0)
     send_y(0)
-    send_z(3)
-    send_z(1)
+    send_z(2, 2)
+    send_z(1, 1)
     wait_y(0)
-    send_z(2)
     up(0)
+    wait_z(2)
+    wait_z(1)
+    wait_y(2)
+    up(2)
     wait_z(3)
-    wait_z(1)
+    wait_y(1)
     wait_y(3)
-    wait_y(1)
     up(3)
-    wait_z(2)
-    wait_y(2)
+    up(1)
     loads[8].wait()
     loads[9].wait()
-    up(2, 1)
-    down(0, 3)
+    down(0, 2)
+    add_core(2)
+    add_core(0)
+    add_y(0)
+    down(3)
     add_core(3)
-    add_core(0)
     add_y(3)
-    add_y(0)
-    down(2)
-    add_core(2)
     down(1)
     add_core(1)
     add_y(2)
@@ -347,7 +372,7 @@
     lasts = []
     for h in range(2):
         total = z_send[0, h].astype(F32)
-        for q in (3, 2, 1):
+        for q in (2, 1):
             lines[q, h].wait_recv()
             total = total + z_in[q, h].astype(F32)
         x_send[h] = total.astype(BF).reshape(2, tok, wide)
@@ -398,11 +423,12 @@
             vm(NZ, 2 * rows, chunk),
             vm(2, NZ * rows, units),
             vm(2, NZ * rows, units),
+            vm(2, 2 * rows, units),
             vm(NZ, 2 * rows, piece),
-            vm(NZ, chunk, piece),
-            vm(NZ, 2, unit, piece),
-            vm(NZ, unit, piece),
-            vm(NZ, unit, piece),
+            vm(NZ, 2, chunk, piece // 2),
+            vm(NZ, 2, 2, unit, piece // 2),
+            vm(NZ, 2, unit, piece // 2),
+            vm(NZ, 2, unit, piece // 2),
             vm(NZ, 2, unit, piece // 2),
             vm(NZ, 2, unit, piece // 2),
             vm(2, 2, tok, piece // 2),
@@ -418,10 +444,10 @@
             dma((NZ, 2)),
             dma((NZ, 2)),
             dma((NZ, 2)),
-            dma((NZ, 2)),
-            dma((NZ, 2)),
-            dma((NZ,)),
-            dma((NZ,)),
+            dma((NZ, 2, 2)),
+            dma((NZ, 2, 2)),
+            dma((NZ, 2)),
+            dma((NZ, 2)),
             dma((NZ, 2)),
             dma((NZ, 2)),
             dma((2,)),

time: 68.3 us -> 72 us (1.054)
  Pallas kernels: 66.6 us -> 70.3 us
    pallas_call x1, Pallas kernels: 66.6 us -> 70.3 us  [fused(): pl.pallas_call(functools.partial(expert_kernel, (tok, cap, piece, units,...]
where the time goes in v5:
time: 72 us; the launch traced here: 71.9 us
  Pallas kernels  70.3 us (98%)
  local copies, waits for them, and re-layouts  1.57 us (2%)
    pallas_call x1, Pallas kernels, fused(): pl.pallas_call(functools.partial(expert_kernel, (tok, cap, piece, units,...  70.3 us
    unnamed x1, local copies, waits for them, and re-layouts  1.57 us

profile of v5, /device:TPU:0, one launch (start us, length us, event | category | flops | bytes accessed | tf_op | source)
XLA Modules:
  0.0 71.9 jit_solution(18027771235133461307)
XLA Ops:
  0.0 70.3 %shard_map.82 = bf16[16,4096]{1,0:T(8,128)(2,1)} custom-call(bf16[16,4096]{1,0:T(8,128)(2,1)} %tokens_hbm.1, s32[8,16]{1,0:T(8,128)} %bitcast.5, f32[8,16]{1,0:T(8,128)} %bitcast.6, s32[1,16]{1,0:T(1,128)} %bitcast.7, bf16[2,2048,1024]{2,1,0:T(8,128)(2,1)} %w_up_hbm.1, bf16[2,1024,2048]{2,1,0:T(8,128)(2,1)} %w_down_hbm.1, bf16[2,64,2048]{2,1,0:T(8,128)(2,1)} %bitcast.4, ...), custom_call_target="tpu_custom_call" | custom-call | tf_op jit(solution)/shard_map/pallas_call | solution.py:406
  70.3 1.6 %copy.10 = bf16[16,4096]{1,0:T(8,128)(2,1)} copy(bf16[16,4096]{1,0:T(8,128)(2,1)} %shard_map.82) | data formatting | bytes 262144

commit v6 on v5

--- a/solution.py
+++ b/solution.py
@@ -47,7 +47,6 @@
     pick,
     part,
     peer,
-    active,
     rows_out,
     y_part,
     core_in,
@@ -223,6 +222,10 @@
         first = ORDER.index(group[0]) * rows
         return slice(first, first + len(group) * rows)
 
+    def send_v(q, j):
+        spot = at_place(q)
+        values[q, j] = go(part.at[j, spot], peer.at[j, spot], v_s.at[q, j], v_r.at[q, j], x_dev)
+
     def up(*group):
         for q in group:
             compact(q)
@@ -249,27 +252,33 @@
                 )
                 value = value + jnp.dot(low, a_out[j, :, at], preferred_element_type=F32)
                 part[j, here, at] = value.astype(BF)
-            for q in group:
-                spot = at_place(q)
-                values[q, j] = go(
-                    part.at[j, spot], peer.at[j, spot], v_s.at[q, j], v_r.at[q, j], x_dev
-                )
+            send_v(group[0], j)
+        for q in group[1:]:
+            for j in range(2):
+                send_v(q, j)
 
     cores, rights, lines = {}, {}, {}
     wide = piece // 2
 
     def down(*group):
         here = span(group)
-        gates_of = []
         for j in range(2):
             for q in group:
                 values[q, j].wait_recv()
             info = packed[j, here, piece:].astype(F32)
             expert = (2 * e + j).astype(F32)
             gate = jnp.where(info[:, 0:8] == expert, info[:, 8:16] + info[:, 16:24], 0.0)
-            gates_of.append(jnp.sum(gate, axis=1, keepdims=True))
+            gate = jnp.sum(gate, axis=1, keepdims=True)
             value = part[j, here].astype(F32) + peer[j, here].astype(F32)
-            active[j, 0 : len(group) * rows] = (value / (1.0 + jnp.exp(-value))).astype(BF)
+            hidden = (value / (1.0 + jnp.exp(-value))).astype(BF)
+            for n in range(0, piece, STEP):
+                at = slice(n, n + STEP)
+                value = jnp.dot(hidden, w_down[j, :, at], preferred_element_type=F32)
+                value = (value * gate).astype(BF)
+                for n_at, q in enumerate(group):
+                    rows_out[q, j * rows : (j + 1) * rows, at] = value[
+                        n_at * rows : (n_at + 1) * rows
+                    ]
         backs = [
             lax.dot_general(
                 equal_iota((chunk, chunk)).astype(BF),
@@ -280,19 +289,6 @@
             for q in group
         ]
         for h in range(2):
-            for n in range(0, wide, STEP):
-                full = slice(h * wide + n, h * wide + n + STEP)
-                for j in range(2):
-                    value = jnp.dot(
-                        active[j, 0 : len(group) * rows],
-                        w_down[j, :, full],
-                        preferred_element_type=F32,
-                    )
-                    value = (value * gates_of[j]).astype(BF)
-                    for n_at, q in enumerate(group):
-                        rows_out[q, j * rows : (j + 1) * rows, full] = value[
-                            n_at * rows : (n_at + 1) * rows
-                        ]
             for q, back in zip(group, backs):
                 for n in range(0, wide, STEP):
                     full = slice(h * wide + n, h * wide + n + STEP)
@@ -354,19 +350,18 @@
     wait_z(3)
     wait_y(1)
     wait_y(3)
-    up(3)
-    up(1)
+    up(3, 1)
     loads[8].wait()
     loads[9].wait()
     down(0, 2)
     add_core(2)
     add_core(0)
-    add_y(0)
     down(3)
     add_core(3)
-    add_y(3)
+    add_y(0)
     down(1)
     add_core(1)
+    add_y(3)
     add_y(2)
     add_y(1)
     lasts = []
@@ -423,7 +418,6 @@
             vm(NZ, 2 * rows, chunk),
             vm(2, NZ * rows, units),
             vm(2, NZ * rows, units),
-            vm(2, 2 * rows, units),
             vm(NZ, 2 * rows, piece),
             vm(NZ, 2, chunk, piece // 2),
             vm(NZ, 2, 2, unit, piece // 2),

time: 72 us -> 65.5 us (0.910)
  Pallas kernels: 70.3 us -> 63.8 us
    pallas_call x1, Pallas kernels: 70.3 us -> 63.8 us  [fused(): pl.pallas_call(functools.partial(expert_kernel, (tok, cap, piece, units,...]
where the time goes in v6:
time: 65.5 us; the launch traced here: 65.4 us
  Pallas kernels  63.8 us (97%)
  local copies, waits for them, and re-layouts  1.57 us (2%)
    pallas_call x1, Pallas kernels, fused(): pl.pallas_call(functools.partial(expert_kernel, (tok, cap, piece, units,...  63.8 us
    unnamed x1, local copies, waits for them, and re-layouts  1.57 us

profile of v6, /device:TPU:0, one launch (start us, length us, event | category | flops | bytes accessed | tf_op | source)
XLA Modules:
  0.0 65.4 jit_solution(13485135305669315446)
XLA Ops:
  0.0 63.8 %shard_map.82 = bf16[16,4096]{1,0:T(8,128)(2,1)} custom-call(bf16[16,4096]{1,0:T(8,128)(2,1)} %tokens_hbm.1, s32[8,16]{1,0:T(8,128)} %bitcast.5, f32[8,16]{1,0:T(8,128)} %bitcast.6, s32[1,16]{1,0:T(1,128)} %bitcast.7, bf16[2,2048,1024]{2,1,0:T(8,128)(2,1)} %w_up_hbm.1, bf16[2,1024,2048]{2,1,0:T(8,128)(2,1)} %w_down_hbm.1, bf16[2,64,2048]{2,1,0:T(8,128)(2,1)} %bitcast.4, ...), custom_call_target="tpu_custom_call" | custom-call | tf_op jit(solution)/shard_map/pallas_call | solution.py:401
  63.8 1.6 %copy.10 = bf16[16,4096]{1,0:T(8,128)(2,1)} copy(bf16[16,4096]{1,0:T(8,128)(2,1)} %shard_map.82) | data formatting | bytes 262144

commit v7 on v6

--- a/solution.py
+++ b/solution.py
@@ -89,7 +89,7 @@
     x_dev = (1 - x, e)
     y_dev = (x, z * 4 + (1 - y) * 2 + c)
     c_dev = (x, z * 4 + y * 2 + (1 - c))
-    z_of = {1: z + 1 - 2 * (z % 2), 2: (z + 2) % 4}
+    z_of = {1: z + 1 - 2 * (z % 2), 2: (z + 2) % 4, 3: 3 - z}
     z_dev = {q: (x, z_of[q] * 4 + y * 2 + c) for q in z_of}
 
     def remote(src, dst, ss, rs, dev):
@@ -146,7 +146,7 @@
     first_out[:, piece:] = meta
     grid[0, half(x), 0:piece] = tokens[:, pl.ds(pl.multiple_of(x * piece, piece), piece)]
     grid[0, half(x), piece:] = meta
-    pl.semaphore_wait(barrier, 5)
+    pl.semaphore_wait(barrier, 6)
 
     sends = []
 
@@ -230,27 +230,32 @@
         for q in group:
             compact(q)
         here = span(group)
+        many = len(group) * rows
         for j in range(2):
             if group[0] == 0:
                 if j == 0:
                     loads[4].wait()
                     loads[5].wait()
                 loads[6 + j].wait()
-            low = lax.dot_general(
-                packed[j, here, 0:piece],
-                a_in[j],
-                (((1,), (1,)), ((), ())),
-                preferred_element_type=F32,
-            )
+            if j == 0:
+                low = lax.dot_general(
+                    packed[:, here, 0:piece].reshape(2 * many, piece),
+                    a_in[...].reshape(2 * cols, piece),
+                    (((1,), (1,)), ((), ())),
+                    preferred_element_type=F32,
+                )
             tenant = packed[j, here, piece + 24 : piece + 25].astype(F32)
-            owner = (lax.broadcasted_iota(jnp.int32, low.shape, 1) // RANK).astype(F32)
-            low = jnp.where(owner == tenant, low, 0.0).astype(BF)
+            owner = lax.broadcasted_iota(jnp.int32, (many, 2 * cols), 1) // RANK
+            owner = (owner - j * (cols // RANK)).astype(F32)
+            mine = jnp.where(owner == tenant, low[j * many : (j + 1) * many], 0.0).astype(BF)
             for n in range(0, units, STEP):
                 at = slice(n, n + STEP)
                 value = jnp.dot(
                     packed[j, here, 0:piece], w_up[j, :, at], preferred_element_type=F32
                 )
-                value = value + jnp.dot(low, a_out[j, :, at], preferred_element_type=F32)
+                value = value + jnp.dot(
+                    mine, a_out[:, :, at].reshape(2 * cols, STEP), preferred_element_type=F32
+                )
                 part[j, here, at] = value.astype(BF)
             send_v(group[0], j)
         for q in group[1:]:
@@ -260,7 +265,7 @@
     cores, rights, lines = {}, {}, {}
     wide = piece // 2
 
-    def down(*group):
+    def down(*group, then=None):
         here = span(group)
         for j in range(2):
             for q in group:
@@ -279,6 +284,8 @@
                     rows_out[q, j * rows : (j + 1) * rows, at] = value[
                         n_at * rows : (n_at + 1) * rows
                     ]
+        if then is not None:
+            then()
         backs = [
             lax.dot_general(
                 equal_iota((chunk, chunk)).astype(BF),
@@ -323,9 +330,6 @@
                 + core_in[q, h, 0].astype(F32)
                 + y_in[q, h].astype(F32)
             )
-            if q == 2:
-                lines[3, h].wait_recv()
-                value = value + z_in[3, h].astype(F32)
             z_send[q, h] = value.astype(BF)
             if q:
                 lines[q, h] = go(
@@ -333,7 +337,7 @@
                     z_in.at[q, h],
                     z_s.at[q, h],
                     z_r.at[q, h],
-                    z_dev[2 if q == 2 else 1],
+                    z_dev[q],
                 )
 
     remote(first_out, grid.at[0, half(1 - x)], tx_s, tx_r, x_dev).wait_recv()
@@ -358,16 +362,15 @@
     add_core(0)
     down(3)
     add_core(3)
+    add_y(2)
     add_y(0)
-    down(1)
+    down(1, then=lambda: add_y(3))
     add_core(1)
-    add_y(3)
-    add_y(2)
     add_y(1)
     lasts = []
     for h in range(2):
         total = z_send[0, h].astype(F32)
-        for q in (2, 1):
+        for q in (2, 3, 1):
             lines[q, h].wait_recv()
             total = total + z_in[q, h].astype(F32)
         x_send[h] = total.astype(BF).reshape(2, tok, wide)

time: 65.5 us -> 63 us (0.962)
  Pallas kernels: 63.8 us -> 61.3 us
    pallas_call x1, Pallas kernels: 63.8 us -> 61.3 us  [fused(): pl.pallas_call(functools.partial(expert_kernel, (tok, cap, piece, units,...]
where the time goes in v7:
time: 63 us; the launch traced here: 62.9 us
  Pallas kernels  61.3 us (97%)
  local copies, waits for them, and re-layouts  1.57 us (2%)
    pallas_call x1, Pallas kernels, fused(): pl.pallas_call(functools.partial(expert_kernel, (tok, cap, piece, units,...  61.3 us
    unnamed x1, local copies, waits for them, and re-layouts  1.57 us

profile of v7, /device:TPU:0, one launch (start us, length us, event | category | flops | bytes accessed | tf_op | source)
XLA Modules:
  0.0 62.9 jit_solution(6646215555447905006)
XLA Ops:
  0.0 61.3 %shard_map.82 = bf16[16,4096]{1,0:T(8,128)(2,1)} custom-call(bf16[16,4096]{1,0:T(8,128)(2,1)} %tokens_hbm.1, s32[8,16]{1,0:T(8,128)} %bitcast.5, f32[8,16]{1,0:T(8,128)} %bitcast.6, s32[1,16]{1,0:T(1,128)} %bitcast.7, bf16[2,2048,1024]{2,1,0:T(8,128)(2,1)} %w_up_hbm.1, bf16[2,1024,2048]{2,1,0:T(8,128)(2,1)} %w_down_hbm.1, bf16[2,64,2048]{2,1,0:T(8,128)(2,1)} %bitcast.4, ...), custom_call_target="tpu_custom_call" | custom-call | tf_op jit(solution)/shard_map/pallas_call | solution.py:404
  61.3 1.6 %copy.10 = bf16[16,4096]{1,0:T(8,128)(2,1)} copy(bf16[16,4096]{1,0:T(8,128)(2,1)} %shard_map.82) | data formatting | bytes 262144
